TPU v7x, 128 devices: a whole 4x4x4 slice. The times are simulated.
128 devices in a mesh: seq: 128 (over x, z, y, core).
Axes of the slice: x: 4, y: 4, z: 4, core: 2. Of those that a mesh axis runs over, the one named last changes fastest.
Arguments:
- tokens: bfloat16 [16384, 1024], P('seq'), may hold values from -24 to 24
- grad_out: bfloat16 [16384, 1024], P('seq'), may hold values from -24 to 24
- w_in: bfloat16 [1024, 4096], replicated, may hold values from -0.1875 to 0.1875
- w_out: bfloat16 [1024, 1024], replicated, may hold values from -0.1875 to 0.1875
- rel_bias: float32 [8, 16], replicated, may hold values from -4 to 4
- send_rows: int32 [128, 128], P('seq'), may hold values from 0 to 127, each once within a row
- recv_place: int32 [128, 128], P('seq'), may hold values from 0 to 127, each once within a row
- block_first: int32 [128], P('seq'), may hold values from 0 to 0, as said below
- user_rows: int32 [128], P('seq'), may hold values from 1 to 128, as said below
- stamps: int32 [16384], P('seq'), may hold values from 0 to 12160, as said below
Outputs:
- out: bfloat16 [16384, 1024], P('seq')
- grad_x: bfloat16 [16384, 1024], P('seq')
- grad_w1: float32 [1024, 4096], P('seq')
- grad_w2: float32 [1024, 1024], P('seq')
Inputs may be any that keep to these rules, and one draw needn't show every extreme that they name: Loader l sends its row send_rows[l, o] to owner o: every owner receives exactly 1 row from every loader. In each owner's row, a permutation: recv_place[o, s] = l + c names the c-th row that loader l sends to owner o. `block_first`: an index among one owner's 1 block; each user holds consecutive blocks of one owner, and an owner's block 0 starts a user. `user_rows`: equal over the blocks of one user, and between (128 times (the user's blocks - 1)) + 1 and 128 times its blocks; some owner holds a single user of 128 rows. `stamps`: never falling along one owner's row slots.
All inputs are finite; a program needn't handle non-finite values.
Results may differ from a plain program's by a relative error of at most 0.0068.
Values may be sent and summed in bfloat16 or wider, within the bound.
A program may use at most 128 MiB of HBM per device.

v0:
```python
import jax
import jax.numpy as jnp
from jax import lax
from jax.sharding import PartitionSpec as P

EPS = 1e-05


def silu_slope(value):
    sigma = jax.nn.sigmoid(value)
    return sigma * (1.0 + value * (1.0 - sigma))


def inverse_of(order):
    length = order.shape[0]
    return jnp.zeros((length,), jnp.int32).at[order].set(jnp.arange(length, dtype=jnp.int32))


def owner_core(activated, own_g, first, live_rows, times, w_out, rel_bias):
    rows_dev = activated.shape[0]
    width = w_out.shape[0]
    heads = rel_bias.shape[0]
    buckets = rel_bias.shape[1]
    block_rows = rows_dev // first.shape[0]
    head_dim = width // heads
    scale = head_dim ** (-0.5)
    row_first = jnp.repeat(first, block_rows) * block_rows
    row_live = jnp.repeat(live_rows, block_rows)
    index = jnp.arange(rows_dev, dtype=jnp.int32)
    alive = index - row_first < row_live
    allowed = (row_first[:, None] == row_first[None, :]) & (index[None, :] <= index[:, None])
    allowed = allowed & alive[:, None] & alive[None, :]
    spread = times[:, None] - times[None, :]
    marks = jnp.left_shift(jnp.int32(1), jnp.arange(buckets - 1, dtype=jnp.int32))
    bucket = jnp.sum((spread[:, :, None] >= marks[None, None, :]).astype(jnp.int32), axis=2)
    onehot = (bucket[:, :, None] == jnp.arange(buckets, dtype=jnp.int32)[None, None, :]).astype(
        jnp.float32
    )
    bias = jnp.einsum("ijb,hb->hij", onehot, rel_bias, precision=lax.Precision.HIGHEST)
    upper = activated[:, :width].astype(jnp.float32)
    values = activated[:, width : 2 * width].reshape(rows_dev, heads, head_dim)
    queries = activated[:, 2 * width : 3 * width].reshape(rows_dev, heads, head_dim)
    keys = activated[:, 3 * width :].reshape(rows_dev, heads, head_dim)
    logits = (
        jnp.einsum("ihd,jhd->hij", queries, keys, preferred_element_type=jnp.float32) * scale + bias
    )
    weights = jnp.where(allowed[None], jax.nn.silu(logits), 0.0).astype(jnp.bfloat16)
    mixed = jnp.einsum("hij,jhd->ihd", weights, values, preferred_element_type=jnp.float32).reshape(
        rows_dev, width
    )
    centre = mixed - jnp.mean(mixed, axis=1, keepdims=True)
    inv_std = lax.rsqrt(jnp.mean(centre * centre, axis=1, keepdims=True) + EPS)
    normed = centre * inv_std
    gated = (normed * upper).astype(jnp.bfloat16)
    layer = lax.dot_general(
        gated, w_out, (((1,), (1,)), ((), ())), preferred_element_type=jnp.float32
    ).astype(jnp.bfloat16)
    grad_gated = jnp.dot(own_g, w_out, preferred_element_type=jnp.float32)
    grad_upper = grad_gated * normed
    grad_normed = grad_gated * upper
    grad_mixed = inv_std * (
        grad_normed
        - jnp.mean(grad_normed, axis=1, keepdims=True)
        - normed * jnp.mean(grad_normed * normed, axis=1, keepdims=True)
    )
    grad_mixed = grad_mixed.astype(jnp.bfloat16).reshape(rows_dev, heads, head_dim)
    grad_values = jnp.einsum(
        "hij,ihd->jhd", weights, grad_mixed, preferred_element_type=jnp.float32
    )
    grad_weights = jnp.einsum(
        "ihd,jhd->hij", grad_mixed, values, preferred_element_type=jnp.float32
    )
    grad_logits = jnp.where(allowed[None], grad_weights * silu_slope(logits), 0.0).astype(
        jnp.bfloat16
    )
    grad_queries = (
        jnp.einsum("hij,jhd->ihd", grad_logits, keys, preferred_element_type=jnp.float32) * scale
    )
    grad_keys = (
        jnp.einsum("hij,ihd->jhd", grad_logits, queries, preferred_element_type=jnp.float32) * scale
    )
    grad_act = jnp.concatenate(
        [
            grad_upper,
            grad_values.reshape(rows_dev, width),
            grad_queries.reshape(rows_dev, width),
            grad_keys.reshape(rows_dev, width),
        ],
        axis=1,
    ).astype(jnp.bfloat16)
    return (layer, gated, grad_act)


def body(
    tokens, grad_out, w_in, w_out, rel_bias, send_rows, recv_place, block_first, user_rows, stamps
):
    devices = lax.axis_size("seq")
    rows_dev = tokens.shape[0]
    share = rows_dev // devices
    send_order = send_rows[0]
    recv_order = recv_place[0]
    send_back = inverse_of(send_order)
    recv_back = inverse_of(recv_order)

    def outbound(value):
        return value[send_order].reshape(devices, share, value.shape[1])

    def inbound(value):
        return value.reshape(rows_dev, value.shape[2])[recv_order]

    def homeward(value):
        return value[recv_back].reshape(devices, share, value.shape[1])

    def arrived(value):
        return value.reshape(rows_dev, value.shape[2])[send_back]

    pre_act = jnp.dot(tokens, w_in, preferred_element_type=jnp.float32)
    activated = jax.nn.silu(pre_act).astype(jnp.bfloat16)
    got_act, got_g = (
        lax.all_to_all(outbound(activated), "seq", split_axis=0, concat_axis=0, tiled=True),
        lax.all_to_all(outbound(grad_out), "seq", split_axis=0, concat_axis=0, tiled=True),
    )
    own_act = inbound(got_act)
    own_g = inbound(got_g)
    layer, gated, grad_act = owner_core(
        own_act, own_g, block_first, user_rows, stamps, w_out, rel_bias
    )
    columns = own_g
    grad_w2 = lax.psum_scatter(
        lax.dot_general(
            columns, gated, (((0,), (0,)), ((), ())), preferred_element_type=jnp.float32
        ),
        "seq",
        scatter_dimension=0,
        tiled=True,
    )
    got_layer, got_back = (
        lax.all_to_all(homeward(layer), "seq", split_axis=0, concat_axis=0, tiled=True),
        lax.all_to_all(homeward(grad_act), "seq", split_axis=0, concat_axis=0, tiled=True),
    )
    layer_home = arrived(got_layer)
    back_home = arrived(got_back)
    grad_pre = (back_home.astype(jnp.float32) * silu_slope(pre_act)).astype(jnp.bfloat16)
    backed = lax.dot_general(
        grad_pre, w_in, (((1,), (1,)), ((), ())), preferred_element_type=jnp.float32
    )
    grad_x = (grad_out.astype(jnp.float32) + backed).astype(jnp.bfloat16)
    columns = tokens
    grad_w1 = lax.psum_scatter(
        lax.dot_general(
            columns, grad_pre, (((0,), (0,)), ((), ())), preferred_element_type=jnp.float32
        ),
        "seq",
        scatter_dimension=0,
        tiled=True,
    )
    out = (tokens.astype(jnp.float32) + layer_home.astype(jnp.float32)).astype(jnp.bfloat16)
    return (out, grad_x, grad_w1, grad_w2)


def solution(mesh):
    placed = (
        P("seq", None),
        P("seq", None),
        P(),
        P(),
        P(),
        P("seq", None),
        P("seq", None),
        P("seq"),
        P("seq"),
        P("seq"),
    )
    return jax.shard_map(
        body,
        mesh=mesh,
        in_specs=placed,
        out_specs=(P("seq", None), P("seq", None), P("seq", None), P("seq", None)),
        check_vma=False,
    )
```

profile of v0, /device:TPU:1, one launch (start us, length us, event | category | flops | bytes accessed | tf_op | source)
XLA Modules:
  0.0 1390.8 jit_solution(10516380602139628616)
XLA Ops:
  8.0 2.0 gather_fusion.4
  11.5 0.9 reshape.353
  12.4 12.0 all-to-all-start.2
  24.3 6.0 multiply_convert_fusion.1
  30.4 2.2 gather_fusion
  32.5 2.7 reduce.3
  35.2 1.6 reshape.349
  36.8 9.8 all-to-all-start
  48.5 1.2 fusion.6
  49.8 2.8 reshape.354
  52.5 1.1 copy.120
  53.7 1.6 gather_fusion.5
  55.2 10.5 all-to-all-done
  65.7 3.4 reshape.350
  69.1 2.7 copy.119
  71.9 2.2 gather_fusion.1
  74.0 1.2 fusion.26
  75.6 0.8 copy.77
  76.4 2.3 select_convert_fusion
  80.0 2.0 copy.83
  82.1 1.7 fusion.16
  83.8 1.1 fusion.11
  84.9 2.8 fusion.28
  87.7 1.0 scatter_custom_fusion
  88.7 1.5 fusion.3
  90.2 1.0 fusion.4
  91.2 1.8 copy.90
  93.2 0.9 copy.91
  94.1 1.2 convolution_convert_fusion
  95.3 0.8 copy.97
  96.2 1.3 pad_maximum_fusion
  97.4 2.2 gather_fusion.6
  99.6 2.7 reduce.6
  102.3 1.6 reshape.355
  103.9 4.7 all-to-all-start.3
  108.6 1.2 scatter_custom_fusion.1
  109.8 18.0 %all-to-all-done.3 = bf16[128,2,2048]{2,1,0:T(2,128)(2,1)S(1)} async-done(((bf16[128,2,2048]{2,1,0:T(2,128)(2,1)}), bf16[128,2,2048]{2,1,0:T(2,128)(2,1)S(1)}, u32[]{:S(2)}, u32[]{:S(2)}) %all-to-all-start.3) | async-done | bytes 1048608 | tf_op jit(solution)/shard_map/all_to_all | solution.py:139
  127.9 3.4 reshape.356
  131.3 2.7 copy.118
  134.0 2.2 gather_fusion.7
  136.2 10.0 convolution_bitcast_fusion
  146.3 17.5 %copy.98 = f32[1024,4096]{1,0:T(8,128)} copy(f32[1024,4096]{0,1:T(8,128)} %convolution_bitcast_fusion) | data formatting | bytes 33554432
  164.7 0.9 gather_fusion.2
  166.6 15.4 %all_to_all.20 = bf16[128,2,512]{2,1,0:T(2,128)(2,1)S(1)} all-to-all(bf16[128,2,512]{2,1,0:T(2,128)(2,1)S(1)} %reshape.351), channel_id=1, replica_groups=mesh['seq'=128] {'seq'}, dimensions={0} | all-to-all | bytes 524288 | tf_op jit(solution)/shard_map/all_to_all | solution.py:138
  182.3 0.9 gather_fusion.3
  183.9 8.0 fusion.2
  191.9 530.3 %reduce-scatter.5.cloned.1.call-done = f32[8,1024]{1,0:T(8,128)} async-done(((f32[1024,1024]{1,0:T(8,128)}), f32[8,1024]{1,0:T(8,128)}) %reduce-scatter.5.cloned.1.call-update) | async-done | bytes 32784 | tf_op jit(solution)/shard_map/reduce_scatter | solution.py:129
  722.2 661.8 %reduce-scatter.7.cloned.1.call-done = f32[8,4096]{1,0:T(8,128)} async-done(((f32[1024,4096]{1,0:T(8,128)}), f32[8,4096]{1,0:T(8,128)}) %reduce-scatter.7.cloned.1.call-update) | async-done | bytes 131088
  (74 shorter events, 7.8 us)
Async XLA Ops:
  7.2 74.9 %copy-start = (bf16[1024,1024]{1,0:T(8,128)(2,1)S(1)}, bf16[1024,1024]{1,0:T(8,128)(2,1)}, u32[]{:S(2)}) copy-start(bf16[1024,1024]{1,0:T(8,128)(2,1)} %param.13) | copy-start | bytes 6291460
  7.2 17.1 %copy-start.7 = (bf16[128,1024]{1,0:T(8,128)(2,1)S(1)}, bf16[128,1024]{1,0:T(8,128)(2,1)}, u32[]{:S(2)}) copy-start(bf16[128,1024]{1,0:T(8,128)(2,1)} %param.10) | copy-start | bytes 786436
  12.4 24.5 %all-to-all-start.2 = ((bf16[128,2,512]{2,1,0:T(2,128)(2,1)}), bf16[128,2,512]{2,1,0:T(2,128)(2,1)}, u32[]{:S(2)}, u32[]{:S(2)}) async-start(bf16[128,2,512]{2,1,0:T(2,128)(2,1)} %reshape.353), calls=%async_computation.2 | async-start | bytes 524288 | tf_op jit(solution)/shard_map/all_to_all | solution.py:121
  32.5 4.3 copy-start.18
  35.2 13.0 copy-start.17
  35.2 13.3 copy-start.16
  36.8 28.8 %all-to-all-start = ((bf16[128,2,2048]{2,1,0:T(2,128)(2,1)}), bf16[128,2,2048]{2,1,0:T(2,128)(2,1)S(1)}, u32[]{:S(2)}, u32[]{:S(2)}) async-start(bf16[128,2,2048]{2,1,0:T(2,128)(2,1)} %reshape.349), calls=%async_computation | async-start | bytes 2097152 | tf_op jit(solution)/shard_map/all_to_all | solution.py:120
  46.6 675.6 %reduce-scatter.5.cloned.1.call-start = ((), (), s32[]{:S(2)}) async-start(), calls=%async_computation.6 | async-start | bytes 4227072 | tf_op jit(solution)/shard_map/reduce_scatter | solution.py:129
  75.4 1.0 copy-start.12
  75.5 0.9 copy-start.10
  76.4 2.3 copy-start.15
  78.7 1.3 copy-start.14
  78.7 3.4 copy-start.2
  78.7 3.4 copy-start.5
  79.0 0.8 copy-start.4
  82.1 1.8 copy-start.3
  82.1 2.8 copy-start.6
  87.7 1.1 copy-start.9
  87.7 2.5 copy-start.13
  88.7 4.3 copy-start.11
  103.9 24.0 %all-to-all-start.3 = ((bf16[128,2,2048]{2,1,0:T(2,128)(2,1)}), bf16[128,2,2048]{2,1,0:T(2,128)(2,1)S(1)}, u32[]{:S(2)}, u32[]{:S(2)}) async-start(bf16[128,2,2048]{2,1,0:T(2,128)(2,1)} %reshape.355), calls=%async_computation.3 | async-start | bytes 2097152 | tf_op jit(solution)/shard_map/all_to_all | solution.py:139
  108.6 1275.4 %reduce-scatter.7.cloned.1.call-start = ((), (), s32[]{:S(2)}) async-start(), calls=%async_computation.7 | async-start | bytes 16908288
  181.9 1.2 copy-start.8
  182.1 1.7 copy-start.1
Sparse Core Ops, SparseCore 0:
  87.8 634.3 reduce-scatter.4
  725.3 658.6 reduce-scatter.6
where the time goes:
time: 1400 us; the launch traced here: 1390 us
  waiting for transfers between devices  1220 us (87%)
  local copies, waits for them, and re-layouts  63.8 us (5%)
  matrix products  37.1 us (3%)
  starting transfers between devices  26.7 us (2%)
  between operations  15.8 us (1%)
  blocking collectives  15.4 us (1%)
    unnamed x3, waiting for transfers between devices  662 us
    reduce_scatter x1, waiting for transfers between devices, body(): lax.psum_scatter(lax.dot_general(columns, gated, (((0,), (0,)), ((), ()))...  530 us
    unnamed x51, local copies, waits for them, and re-layouts  39.1 us
  transfers between devices with their start and end apart: 5, of which 4 were waited for; matrix products, arithmetic and copies ran while one was open for 6% of the time, Pallas kernels for 0%

commit v1 on v0

v1 whole, which is shorter than its diff:
```python
import functools

import jax
import jax.numpy as jnp
from jax import lax
from jax.experimental import pallas as pl
from jax.experimental.pallas import tpu as pltpu
from jax.sharding import PartitionSpec as P

EPS = 1e-05
F32, BF16 = jnp.float32, jnp.bfloat16
MESH = pl.DeviceIdType.MESH
ORDERS = ((0, 0, 1, 2), (0, 1, 1, 2), (0, 1, 2, 2), (0, 0, 1, 2), (0, 1, 1, 2))
COUNT = tuple(sum(row.count(o) for row in ORDERS) for o in range(3))


def slots(block, order):
    start = sum(row.count(order) for row in ORDERS[:block])
    return start, ORDERS[block].count(order)


def dot(a, b, dims=((1,), (0,))):
    return lax.dot_general(a, b, (dims, ((), ())), preferred_element_type=F32)


def kernel(
    tok, gout, w_in, w_out, relb, srow, rplace, first, live, stamps,
    out, gx, gw1, gw2,
    wi, wo, sa, ra, sb, xg, meta, bias, mask, xv, gv, xt, gt, act, slp, pw, ps, mix, gg,
    stat, ga, gm, gp, b0, b1, b2, r10, r11, r12, s10, s11, s12, r20, r21, r22, s20, s21, s22,
    r30, r31, r32, fin, rfin, part, rpart, ret, ry, sz, rz,
    wsem, a_s, a_r, y_s, y_r, c_s, c_r, m_s, m_r, t_s, t_r, p1_s, p1_r, p2_s, p2_r, p3_s, p3_r,
    f_s, f_r, q_s, q_r, v_s, v_r, z_s, z_r,
):
    bs, r1, s1, r2 = (b0, b1, b2), (r10, r11, r12), (s10, s11, s12), (r20, r21, r22)
    s2, r3 = (s20, s21, s22), (r30, r31, r32)
    me = lax.axis_index("seq")
    c = lax.rem(me, 2)
    y = lax.rem(me // 2, 4)
    z = lax.rem(me // 8, 4)
    x = me // 32
    xz = me // 8
    low = lax.rem(me, 8)
    mate = me + 1 - 2 * c
    coords, strides = (x, z, y), (32, 8, 2)

    def along(axis, k):
        there = lax.rem(coords[axis] + k, 4)
        return there, me + (there - coords[axis]) * strides[axis]

    def rcopy(src, dst, send, recv, dev):
        return pltpu.make_async_remote_copy(
            src_ref=src, dst_ref=dst, send_sem=send, recv_sem=recv,
            device_id=(dev,), device_id_type=MESH,
        )

    barrier = pltpu.get_barrier_semaphore()

    @pl.loop(1, 16)
    def _(k):
        pl.semaphore_signal(
            barrier, inc=1, device_id=(lax.rem(xz + k, 16) * 8 + low,), device_id_type=MESH
        )

    for k in range(1, 4):
        pl.semaphore_signal(barrier, inc=1, device_id=(along(2, k)[1],), device_id_type=MESH)
    pl.semaphore_signal(barrier, inc=1, device_id=(mate,), device_id_type=MESH)

    half = pl.multiple_of(c * 512, 512)
    loads = [
        pltpu.make_async_copy(w_in.at[:, pl.ds(f * 1024 + half, 512)], wi.at[f], wsem.at[f])
        for f in range(4)
    ]
    loads.append(pltpu.make_async_copy(w_out.at[:, pl.ds(half, 512)], wo, wsem.at[4]))
    for load in loads:
        load.start()

    rows = lax.broadcasted_iota(jnp.int32, (128, 128), 0)
    lanes = lax.broadcasted_iota(jnp.int32, (128, 128), 1)
    eye = rows == lanes

    def to_column(row):
        return jnp.sum(jnp.where(eye, row, 0.0), axis=1, keepdims=True)

    def to_row(column):
        return jnp.sum(jnp.where(eye, column, 0.0), axis=0, keepdims=True)

    wanted = to_column(srow[...].astype(F32))
    pick = jnp.where(wanted == lanes.astype(F32), 1.0, 0.0).astype(BF16)
    sent = jnp.concatenate(
        [dot(pick, tok[...]).reshape(16, 8, 1024), dot(pick, gout[...]).reshape(16, 8, 1024)],
        axis=1,
    )
    sa[...] = sent.astype(BF16)

    pl.semaphore_wait(barrier, 19)

    @pl.loop(1, 16)
    def _(k):
        to = lax.rem(xz + k, 16)
        rcopy(sa.at[to], ra.at[xz], a_s.at[k], a_r.at[k], to * 8 + low).start()

    ra[xz] = sa[xz]

    m = rplace[...]
    place = (m & 1) * 64 + ((m >> 1) & 3) * 16 + (m >> 5) * 4 + ((m >> 3) & 3)
    lands = place == rows
    slot = to_row(jnp.sum(jnp.where(lands, lanes.astype(F32), 0.0), axis=1, keepdims=True))
    when = to_row(jnp.sum(jnp.where(lands, stamps[...].astype(F32), 0.0), axis=1, keepdims=True))
    alive = slot < (live[0] + first[0] * 128).astype(F32)
    sub = lax.broadcasted_iota(jnp.int32, (8, 128), 0)
    meta[c] = jnp.where(
        sub == 0,
        jnp.where(alive, slot, 1e6),
        jnp.where(sub == 1, jnp.where(alive, slot, -1.0), when),
    )
    meta_copy = rcopy(meta.at[c], meta.at[c], m_s, m_r, mate)
    meta_copy.start()

    def wait_meta():
        rcopy(meta.at[1 - c], meta.at[1 - c], m_s, m_r, mate).wait_recv()

    wait_meta()
    for o in range(2):
        keys, asks, times = meta[o, 0:1], to_column(meta[o, 1:2]), meta[o, 2:3]
        mask[o] = jnp.where(keys <= asks, 1.0, 0.0)
        spread = to_column(times) - times

        @pl.loop(0, 4)
        def _(h, o=o, spread=spread):
            value = jnp.full((128, 128), relb[4 * c + h, 0], F32)
            for k in range(15):
                value = jnp.where(spread >= float(2**k), relb[4 * c + h, k + 1], value)
            bias[4 * o + h] = value

    @pl.loop(1, 16)
    def _(k):
        come = lax.rem(xz + 16 - k, 16)
        rcopy(sa.at[come], ra.at[come], a_s.at[k], a_r.at[k], come * 8 + low).wait_recv()

    r256 = lax.broadcasted_iota(jnp.int32, (256, 256), 0)
    l256 = lax.broadcasted_iota(jnp.int32, (256, 256), 1)

    def swapped(r):
        return (r & 15) * 16 + ((r >> 5) & 1) * 8 + (r >> 6) * 2 + ((r >> 4) & 1)

    turn = jnp.where(l256 == swapped(r256), 1.0, 0.0).astype(BF16)
    sb[...] = dot(turn, ra[...].reshape(256, 1024)).astype(BF16).reshape(4, 2, 2, 16, 1024)
    for k in range(1, 4):
        to, dev = along(2, k)
        rcopy(sb.at[to], xg.at[c, y], y_s.at[k], y_r.at[k], dev).start()
    xg[c, y] = sb[y]
    rcopy(xg.at[c, y], xg.at[c, y], c_s.at[0], c_r.at[0], mate).start()
    for k in range(1, 4):
        come = lax.rem(y + 4 - k, 4)
        rcopy(sb.at[come], xg.at[c, come], y_s.at[k], y_r.at[k], me).wait_recv()
        rcopy(xg.at[c, come], xg.at[c, come], c_s.at[k], c_r.at[k], mate).start()
    for k in range(4):
        come = lax.rem(y + 4 - k, 4)
        rcopy(xg.at[1 - c, come], xg.at[1 - c, come], c_s.at[k], c_r.at[k], mate).wait_recv()

    for o in range(2):
        xv[128 * o : 128 * o + 128] = xg[:, :, 0, o].reshape(128, 1024)
        gv[128 * o : 128 * o + 128] = xg[:, :, 1, o].reshape(128, 1024)

    for load in loads:
        load.wait()

    for f in range(4):
        pre = dot(xv[...], wi[f])
        sig = jax.nn.sigmoid(pre)
        act[f] = (pre * sig).astype(BF16)
        slp[f] = sig * (1.0 + pre * (1.0 - sig))
    gg[...] = dot(gv[...], wo[...])
    heads = [(o, h) for o in range(2) for h in range(4)]
    scale = 128**-0.5
    for o, h in heads:
        here = (slice(128 * o, 128 * o + 128), slice(128 * h, 128 * h + 128))
        v, q, k = (act[(f,) + here] for f in (1, 2, 3))
        logits = dot(q, k, ((1,), (1,))) * scale + bias[4 * o + h]
        sig = jax.nn.sigmoid(logits)
        allowed = mask[o] > 0.5
        w = jnp.where(allowed, logits * sig, 0.0).astype(BF16)
        pw[4 * o + h] = w
        ps[4 * o + h] = jnp.where(allowed, sig * (1.0 + logits * (1.0 - sig)), 0.0)
        mix[here] = dot(w, v)

    gn = gg[...] * act[0].astype(F32)
    mixed = mix[...]
    total = jnp.sum(mixed, axis=1, keepdims=True)
    centre = mixed - total * (1.0 / 512)
    square = jnp.sum(centre * centre, axis=1, keepdims=True)
    gsum = jnp.sum(gn, axis=1, keepdims=True)
    gdot = jnp.sum(gn * centre, axis=1, keepdims=True)
    col = lax.broadcasted_iota(jnp.int32, (256, 128), 1)
    stat[c] = jnp.where(
        col == 0, total, jnp.where(col == 1, square, jnp.where(col == 2, gsum, gdot))
    )
    stat_copy = rcopy(stat.at[c], stat.at[c], t_s, t_r, mate)
    stat_copy.start()
    xt[...] = xv[...].T
    gt[...] = gv[...].T
    rcopy(stat.at[1 - c], stat.at[1 - c], t_s, t_r, mate).wait_recv()
    theirs = stat[1 - c]
    total2, square2, gsum2, gdot2 = (theirs[:, i : i + 1] for i in range(4))
    mean = (total + total2) * (1.0 / 1024)
    off, off2 = total * (1.0 / 512) - mean, total2 * (1.0 / 512) - mean
    var = (square + square2 + 512.0 * (off * off + off2 * off2)) * (1.0 / 1024)
    inv_std = lax.rsqrt(var + EPS)
    mean_gn = (gsum + gsum2) * (1.0 / 1024)
    mean_gnn = (gdot + off * gsum + gdot2 + off2 * gsum2) * inv_std * (1.0 / 1024)
    normed = (mix[...] - mean) * inv_std
    upper = act[0].astype(F32)
    ga[...] = (normed * upper).astype(BF16)
    ggv = gg[...]
    gm[...] = (inv_std * (ggv * upper - mean_gn - normed * mean_gnn)).astype(BF16)
    gp[0] = ((ggv * normed).astype(BF16).astype(F32) * slp[0]).astype(BF16)

    def product(block, left, right):
        @pl.loop(0, 4)
        def _(i):
            rows = pl.ds(pl.multiple_of(i * 256, 256), 256)
            tile = dot(left[rows, :], right).astype(BF16)
            seen = [0, 0, 0]
            for j in range(4):
                o = ORDERS[block][j]
                at = slots(block, o)[0] + seen[o]
                seen[o] += 1
                part4 = tile[:, 128 * j : 128 * j + 128].reshape(4, 4, 16, 128)
                if o == 0:
                    bs[0][at, i] = part4
                elif o == 1:
                    bs[1][at, :, :, i] = part4
                else:
                    for k in range(4):
                        bs[2][at, :, i, k] = part4[k]

    def hop(stage, block, o, k):
        axis = (o + stage) % 3
        there, dev = along(axis, k)
        if stage < 2:
            start, count = slots(block, o)
            at = pl.ds(start, count)
            i = (block * 3 + o) * 3 + k - 1
            src, dst = ((bs, r1), (s1, r2))[stage]
            send, recv = ((p1_s, p1_r), (p2_s, p2_r))[stage]
            return rcopy(
                src[o].at[at, there], dst[o].at[k - 1, at], send.at[i], recv.at[i], dev
            )
        i = o * 3 + k - 1
        return rcopy(s2[o].at[:, there], r3[o].at[k - 1], p3_s.at[i], p3_r.at[i], dev)

    def send(stage, block):
        for k in (2, 1, 3):
            for o in range(3):
                hop(stage, block, o, k).start()

    def add(stage, block):
        for o in range(3):
            for k in range(1, 4):
                hop(stage, block, o, k).wait_recv()
            here = coords[(o + stage) % 3]
            start, count = slots(block, o)
            at = slice(start, start + count)
            if stage == 0:
                value = bs[o][at, here].astype(F32)
                for k in range(3):
                    value = value + r1[o][k, at].astype(F32)
                s1[o][at] = value.astype(BF16)
            else:
                value = s1[o][at, here].astype(F32)
                for k in range(3):
                    value = value + r2[o][k, at].astype(F32)
                s2[o][at] = value.astype(BF16)

    product(0, gt, ga[...])
    send(0, 0)
    product(1, xt, gp[0])
    send(0, 1)
    part[0] = dot(ga[...], wo[...], ((1,), (1,))).reshape(2, 2, 64, 1024)

    for o, h in heads:
        here = (slice(128 * o, 128 * o + 128), slice(128 * h, 128 * h + 128))
        v, q, k = (act[(f,) + here] for f in (1, 2, 3))
        gmh, w = gm[here], pw[4 * o + h]
        gl = (dot(gmh, v, ((1,), (1,))) * ps[4 * o + h]).astype(BF16)
        grads = (
            dot(w, gmh, ((0,), (0,))),
            dot(gl, k) * scale,
            dot(gl, q, ((0,), (0,))) * scale,
        )
        for f in (1, 2, 3):
            gp[(f,) + here] = (
                grads[f - 1].astype(BF16).astype(F32) * slp[(f,) + here]
            ).astype(BF16)

    product(2, xt, gp[1])
    send(0, 2)
    product(3, xt, gp[2])
    send(0, 3)
    product(4, xt, gp[3])
    send(0, 4)
    back = dot(gp[0], wi[0], ((1,), (1,)))
    for f in range(1, 4):
        back = back + dot(gp[f], wi[f], ((1,), (1,)))
    part[1] = back.reshape(2, 2, 64, 1024)
    core = rcopy(part.at[:, :, 1 - c], rpart, q_s, q_r, mate)
    core.start()
    core.wait_recv()
    for o in range(2):
        layer = (part[0, o, c] + rpart[0, o]).astype(BF16)
        grad = xg[c, :, 1, o].astype(F32) + (part[1, o, c] + rpart[1, o]).reshape(4, 16, 1024)
        ret[:, 0, o] = layer.reshape(4, 16, 1024)
        ret[:, 1, o] = grad.astype(BF16)
    for k in range(1, 4):
        to, dev = along(2, k)
        rcopy(ret.at[to], ry.at[y], v_s.at[k], v_r.at[k], dev).start()
    ry[y] = ret[y]
    add(0, 0)
    send(1, 0)
    for k in range(1, 4):
        come = lax.rem(y + 4 - k, 4)
        rcopy(ret.at[come], ry.at[come], v_s.at[k], v_r.at[k], me).wait_recv()
    unturn = jnp.where(r256 == swapped(l256), 1.0, 0.0).astype(BF16)
    sz[...] = dot(unturn, ry[...].reshape(256, 1024)).astype(BF16).reshape(16, 16, 1024)

    @pl.loop(1, 16)
    def _(k):
        to = lax.rem(xz + k, 16)
        rcopy(sz.at[to], rz.at[xz], z_s.at[k], z_r.at[k], to * 8 + low).start()

    rz[xz] = sz[xz]
    for block in range(1, 5):
        add(0, block)
        send(1, block)

    @pl.loop(1, 16)
    def _(k):
        come = lax.rem(xz + 16 - k, 16)
        rcopy(sz.at[come], rz.at[come], z_s.at[k], z_r.at[k], come * 8 + low).wait_recv()

    got = rz[...].astype(F32)
    unpick = jnp.where(srow[...] == rows, 1.0, 0.0).astype(BF16)
    layer = dot(unpick, got[:, :8].reshape(128, 1024).astype(BF16))
    out[...] = (tok[...].astype(F32) + layer).astype(BF16)
    gx[...] = dot(unpick, got[:, 8:].reshape(128, 1024).astype(BF16)).astype(BF16)

    for block in range(5):
        add(1, block)
    for k in (2, 1, 3):
        for o in range(3):
            hop(2, 0, o, k).start()
    for o in range(3):
        for k in range(1, 4):
            hop(2, 0, o, k).wait_recv()
        value = s2[o][:, coords[(o + 2) % 3]].astype(F32)
        for k in range(3):
            value = value + r3[o][k].astype(F32)
        for block in range(5):
            start, _ = slots(block, o)
            mine = [j for j in range(4) if ORDERS[block][j] == o]
            for n, j in enumerate(mine):
                fin[4 * block + j] = value[start + n]
    away, home = pl.multiple_of(8 * (1 - c), 8), pl.multiple_of(8 * c, 8)
    last = rcopy(fin.at[:, pl.ds(away, 8)], rfin, f_s, f_r, mate)
    last.start()
    other = pl.multiple_of(512 - half, 512)
    mine = fin[:, pl.ds(home, 8)]
    for j in range(4):
        gw2[:, pl.ds(half + 128 * j, 128)] = mine[j]
        for f in range(4):
            gw1[:, pl.ds(f * 1024 + half + 128 * j, 128)] = mine[4 + 4 * f + j]
    last.wait_recv()
    for j in range(4):
        gw2[:, pl.ds(other + 128 * j, 128)] = rfin[j]
        for f in range(4):
            gw1[:, pl.ds(f * 1024 + other + 128 * j, 128)] = rfin[4 + 4 * f + j]

    @pl.loop(1, 16)
    def _(k):
        to = lax.rem(xz + k, 16)
        rcopy(sa.at[to], ra.at[xz], a_s.at[k], a_r.at[k], to * 8 + low).wait_send()
        rcopy(sz.at[to], rz.at[xz], z_s.at[k], z_r.at[k], to * 8 + low).wait_send()

    meta_copy.wait_send()
    stat_copy.wait_send()
    core.wait_send()
    last.wait_send()
    for k in range(4):
        come = lax.rem(y + 4 - k, 4)
        rcopy(xg.at[c, come], xg.at[c, come], c_s.at[k], c_r.at[k], mate).wait_send()
    for k in range(1, 4):
        to, dev = along(2, k)
        rcopy(sb.at[to], xg.at[c, y], y_s.at[k], y_r.at[k], dev).wait_send()
        rcopy(ret.at[to], ry.at[y], v_s.at[k], v_r.at[k], dev).wait_send()
        for o in range(3):
            for block in range(5):
                hop(0, block, o, k).wait_send()
                hop(1, block, o, k).wait_send()
            hop(2, 0, o, k).wait_send()


def body(
    tokens, grad_out, w_in, w_out, rel_bias, send_rows, recv_place, block_first, user_rows, stamps
):
    vmem, smem = pl.BlockSpec(memory_space=pltpu.VMEM), pl.BlockSpec(memory_space=pltpu.SMEM)
    hbm = pl.BlockSpec(memory_space=pl.ANY)
    dma = pltpu.SemaphoreType.DMA

    def v(shape, kind=BF16):
        return pltpu.VMEM(shape, kind)

    scratch = [
        v((4, 1024, 512)), v((1024, 512)), v((16, 16, 1024)), v((16, 16, 1024)),
        v((4, 2, 2, 16, 1024)), v((2, 4, 2, 2, 16, 1024)), v((2, 8, 128), F32),
        v((8, 128, 128), F32), v((2, 128, 128), F32), v((256, 1024)), v((256, 1024)),
        v((1024, 256)), v((1024, 256)), v((4, 256, 512)), v((4, 256, 512), F32),
        v((8, 128, 128)), v((8, 128, 128), F32), v((256, 512), F32), v((256, 512), F32),
        v((2, 256, 128), F32), v((256, 512)), v((256, 512)), v((4, 256, 512)),
    ]
    scratch += [v((n, 4, 4, 4, 16, 128)) for n in COUNT]
    scratch += [v((3, n, 4, 4, 16, 128)) for n in COUNT]
    scratch += [v((n, 4, 4, 16, 128)) for n in COUNT]
    scratch += [v((3, n, 4, 16, 128)) for n in COUNT]
    scratch += [v((n, 4, 16, 128)) for n in COUNT]
    scratch += [v((3, n, 16, 128)) for n in COUNT]
    scratch += [
        v((20, 16, 128), F32), v((20, 8, 128), F32), v((2, 2, 2, 64, 1024), F32),
        v((2, 2, 64, 1024), F32), v((4, 2, 2, 16, 1024)), v((4, 2, 2, 16, 1024)),
        v((16, 16, 1024)), v((16, 16, 1024)),
    ]
    scratch += [dma((5,)), dma((16,)), dma((16,)), dma((4,)), dma((4,)), dma((4,)), dma((4,))]
    scratch += [dma, dma, dma, dma, dma((45,)), dma((45,)), dma((45,)), dma((45,))]
    scratch += [dma((9,)), dma((9,)), dma, dma, dma, dma, dma((4,)), dma((4,)), dma((16,)), dma((16,))]
    return tuple(
        pl.pallas_call(
            kernel,
            out_shape=(
                jax.ShapeDtypeStruct((128, 1024), BF16),
                jax.ShapeDtypeStruct((128, 1024), BF16),
                jax.ShapeDtypeStruct((8, 4096), F32),
                jax.ShapeDtypeStruct((8, 1024), F32),
            ),
            in_specs=[vmem, vmem, hbm, hbm, smem, vmem, vmem, smem, smem, vmem],
            out_specs=(vmem, vmem, vmem, vmem),
            scratch_shapes=scratch,
            compiler_params=pltpu.CompilerParams(
                collective_id=0, has_side_effects=True, vmem_limit_bytes=56 * 2**20
            ),
        )(
            tokens, grad_out, w_in, w_out, rel_bias, send_rows, recv_place, block_first,
            user_rows, stamps.reshape(1, 128),
        )
    )


def solution(mesh):
    placed = (
        P("seq", None), P("seq", None), P(), P(), P(), P("seq", None), P("seq", None),
        P("seq"), P("seq"), P("seq"),
    )
    return jax.shard_map(
        body,
        mesh=mesh,
        in_specs=placed,
        out_specs=(P("seq", None), P("seq", None), P("seq", None), P("seq", None)),
        check_vma=False,
    )
```

time: 1400 us -> 86.6 us (0.06)
  waiting for transfers between devices: 1220 us -> 0 us
  Pallas kernels: 0 us -> 78.1 us
  local copies, waits for them, and re-layouts: 63.8 us -> 6.28 us
  matrix products: 37.1 us -> 0 us
  starting transfers between devices: 26.7 us -> 0 us
  blocking collectives: 15.4 us -> 0 us
    unnamed x3 -> x0, waiting for transfers between devices: 662 us -> none
    reduce_scatter x1 -> x0, waiting for transfers between devices: 530 us -> none  [body(): lax.psum_scatter(lax.dot_general(columns, gated, (((0,), (0,)), ((), ()))...]
    pallas_call x0 -> x1, Pallas kernels: none -> 78.1 us  [body(): pl.pallas_call(kernel, out_shape=(jax.ShapeDtypeStruct((128, 1024), BF16)...]
    dot_general x13 -> x0, matrix products: 37.1 us -> none  [the longest x1 10 us: body(): lax.dot_general(columns, grad_pre, (((0,), (0,)), ((), ())), preferred_el...]
    unnamed x51 -> x4, local copies, waits for them, and re-layouts: 39.1 us -> 6.28 us
    all_to_all x3 -> x0, waiting for transfers between devices: 28.5 us -> none  [the longest x1 18 us: body(): lax.all_to_all(homeward(grad_act), 'seq', split_axis=0, concat_axis=0, ti...]
    all_to_all x3 -> x0, starting transfers between devices: 26.4 us -> none  [the longest x1 12 us: body(): lax.all_to_all(outbound(grad_out), 'seq', split_axis=0, concat_axis=0, ti...]
    all_to_all x1 -> x0, blocking collectives: 15.4 us -> none  [body(): lax.all_to_all(homeward(layer), 'seq', split_axis=0, concat_axis=0, tiled...]
  transfers between devices with their start and end apart: 5 -> 0, of which waited for: 4 -> 0; matrix products, arithmetic and copies ran while one was open for 6% -> 0% of each run, Pallas kernels for 0% -> 0%
where the time goes in v1:
time: 86.6 us; the launch traced here: 86.3 us
  Pallas kernels  78.1 us (90%)
  local copies, waits for them, and re-layouts  6.28 us (7%)
  between operations  1.93 us (2%)
    pallas_call x1, Pallas kernels, body(): pl.pallas_call(kernel, out_shape=(jax.ShapeDtypeStruct((128, 1024), BF16)...  78.1 us
    unnamed x4, local copies, waits for them, and re-layouts  6.28 us

profile of v1, /device:TPU:1, one launch (start us, length us, event | category | flops | bytes accessed | tf_op | source)
XLA Modules:
  0.0 86.3 jit_solution(13132536325707272194)
XLA Ops:
  1.9 78.1 %shard_map.129 = (bf16[128,1024]{1,0:T(8,128)(2,1)}, bf16[128,1024]{1,0:T(8,128)(2,1)}, f32[8,4096]{1,0:T(8,128)}, f32[8,1024]{1,0:T(8,128)}) custom-call(bf16[128,1024]{1,0:T(8,128)(2,1)} %tok.1, bf16[128,1024]{1,0:T(8,128)(2,1)} %gout.1, bf16[1024,4096]{1,0:T(8,128)(2,1)} %w_in.1, bf16[1024,1024]{1,0:T(8,128)(2,1)} %w_out.1, f32[8,16]{1,0:T(8,128)} %relb.1, ...), custom_call_target="tpu_custom_call" | custom-call | tf_op jit(solution)/shard_map/pallas_call | solution.py:436
  80.0 1.7 %copy.20 = bf16[128,1024]{1,0:T(8,128)(2,1)} copy(bf16[128,1024]{1,0:T(8,128)(2,1)} %get-tuple-element.8) | data formatting | bytes 524288
  81.7 1.7 %copy.21 = bf16[128,1024]{1,0:T(8,128)(2,1)} copy(bf16[128,1024]{1,0:T(8,128)(2,1)} %get-tuple-element.9) | data formatting | bytes 524288
  83.3 1.6 %copy.22 = f32[8,4096]{1,0:T(8,128)} copy(f32[8,4096]{1,0:T(8,128)} %get-tuple-element.10) | data formatting | bytes 262144
  84.9 1.4 %copy.23 = f32[8,1024]{1,0:T(8,128)} copy(f32[8,1024]{1,0:T(8,128)} %get-tuple-element.11) | data formatting | bytes 65536

commit v2 on v1

--- a/solution.py
+++ b/solution.py
@@ -26,11 +26,11 @@
 def kernel(
     tok, gout, w_in, w_out, relb, srow, rplace, first, live, stamps,
     out, gx, gw1, gw2,
-    wi, wo, sa, ra, sb, xg, meta, bias, mask, xv, gv, xt, gt, act, slp, pw, ps, mix, gg,
+    wi, wo, sf, sa, rg, rf, meta, bias, mask, xv, gv, xt, gt, act, slp, pw, ps, mix, gg,
     stat, ga, gm, gp, b0, b1, b2, r10, r11, r12, s10, s11, s12, r20, r21, r22, s20, s21, s22,
-    r30, r31, r32, fin, rfin, part, rpart, ret, ry, sz, rz,
-    wsem, a_s, a_r, y_s, y_r, c_s, c_r, m_s, m_r, t_s, t_r, p1_s, p1_r, p2_s, p2_r, p3_s, p3_r,
-    f_s, f_r, q_s, q_r, v_s, v_r, z_s, z_r,
+    r30, r31, r32, fin, rfin, part, rpart, rz,
+    wsem, a_s, a_r, c_s, c_r, m_s, m_r, t_s, t_r, p1_s, p1_r, p2_s, p2_r, p3_s, p3_r,
+    f_s, f_r, q_s, q_r, z_s, z_r,
 ):
     bs, r1, s1, r2 = (b0, b1, b2), (r10, r11, r12), (s10, s11, s12), (r20, r21, r22)
     s2, r3 = (s20, s21, s22), (r30, r31, r32)
@@ -39,8 +39,7 @@
     y = lax.rem(me // 2, 4)
     z = lax.rem(me // 8, 4)
     x = me // 32
-    xz = me // 8
-    low = lax.rem(me, 8)
+    chip = me // 2
     mate = me + 1 - 2 * c
     coords, strides = (x, z, y), (32, 8, 2)
 
@@ -56,14 +55,12 @@
 
     barrier = pltpu.get_barrier_semaphore()
 
-    @pl.loop(1, 16)
+    @pl.loop(1, 64)
     def _(k):
         pl.semaphore_signal(
-            barrier, inc=1, device_id=(lax.rem(xz + k, 16) * 8 + low,), device_id_type=MESH
+            barrier, inc=1, device_id=(lax.rem(chip + k, 64) * 2 + c,), device_id_type=MESH
         )
 
-    for k in range(1, 4):
-        pl.semaphore_signal(barrier, inc=1, device_id=(along(2, k)[1],), device_id_type=MESH)
     pl.semaphore_signal(barrier, inc=1, device_id=(mate,), device_id_type=MESH)
 
     half = pl.multiple_of(c * 512, 512)
@@ -85,25 +82,58 @@
     def to_row(column):
         return jnp.sum(jnp.where(eye, column, 0.0), axis=0, keepdims=True)
 
-    wanted = to_column(srow[...].astype(F32))
+    order = ((rows & 63) << 1) + (rows >> 6)
+    wanted = jnp.sum(
+        jnp.where(lanes == order, srow[...].astype(F32), 0.0), axis=1, keepdims=True
+    )
     pick = jnp.where(wanted == lanes.astype(F32), 1.0, 0.0).astype(BF16)
-    sent = jnp.concatenate(
-        [dot(pick, tok[...]).reshape(16, 8, 1024), dot(pick, gout[...]).reshape(16, 8, 1024)],
-        axis=1,
-    )
-    sa[...] = sent.astype(BF16)
-
-    pl.semaphore_wait(barrier, 19)
-
-    @pl.loop(1, 16)
-    def _(k):
-        to = lax.rem(xz + k, 16)
-        rcopy(sa.at[to], ra.at[xz], a_s.at[k], a_r.at[k], to * 8 + low).start()
-
-    ra[xz] = sa[xz]
+
+    def fold(value, kind):
+        for o in range(2):
+            for j in range(8):
+                sf[pl.ds(kind * 16 + o * 8 + j, 64, stride=32), :] = value[
+                    64 * o : 64 * o + 64, 128 * j : 128 * j + 128
+                ]
+
+    def unfolded(ref, kind, o):
+        return jnp.concatenate(
+            [ref[pl.ds(kind * 16 + o * 8 + j, 64, stride=32), :] for j in range(8)], axis=1
+        )
+
+    fold(dot(pick, tok[...]), 0)
+    fold(dot(pick, gout[...]), 1)
+    sa[...] = sf[...].reshape(64, 32, 128).astype(BF16)
+
+    pl.semaphore_wait(barrier, 64)
+
+    def peer(i, j):
+        there = lax.rem(x + i, 4) * 16 + lax.rem(z * 4 + y + j, 16)
+        return there, there * 2 + c
+
+    def scatter(src, dst, sends, recvs):
+        @pl.loop(0, 16)
+        def _(j):
+            for i in range(4):
+                there, dev = peer(i, j)
+
+                def go():
+                    rcopy(src.at[there], dst.at[chip], sends.at[i], recvs.at[i], dev).start()
+
+                if i == 0:
+                    pl.when(j > 0)(go)
+                else:
+                    go()
+
+    def scattered(src, dst, sends, recvs, i):
+        come = lax.rem(x + 4 - i, 4) * 16
+        at = pl.ds(come, 16 if i else 15)
+        return rcopy(src.at[at], dst.at[at], sends.at[i], recvs.at[i], mate)
+
+    scatter(sa, rg.at[c], a_s, a_r)
+    rg[c, chip] = sa[chip]
 
     m = rplace[...]
-    place = (m & 1) * 64 + ((m >> 1) & 3) * 16 + (m >> 5) * 4 + ((m >> 3) & 3)
+    place = (m & 1) * 64 + (m >> 1)
     lands = place == rows
     slot = to_row(jnp.sum(jnp.where(lands, lanes.astype(F32), 0.0), axis=1, keepdims=True))
     when = to_row(jnp.sum(jnp.where(lands, stamps[...].astype(F32), 0.0), axis=1, keepdims=True))
@@ -133,35 +163,28 @@
                 value = jnp.where(spread >= float(2**k), relb[4 * c + h, k + 1], value)
             bias[4 * o + h] = value
 
-    @pl.loop(1, 16)
-    def _(k):
-        come = lax.rem(xz + 16 - k, 16)
-        rcopy(sa.at[come], ra.at[come], a_s.at[k], a_r.at[k], come * 8 + low).wait_recv()
-
-    r256 = lax.broadcasted_iota(jnp.int32, (256, 256), 0)
-    l256 = lax.broadcasted_iota(jnp.int32, (256, 256), 1)
-
-    def swapped(r):
-        return (r & 15) * 16 + ((r >> 5) & 1) * 8 + (r >> 6) * 2 + ((r >> 4) & 1)
-
-    turn = jnp.where(l256 == swapped(r256), 1.0, 0.0).astype(BF16)
-    sb[...] = dot(turn, ra[...].reshape(256, 1024)).astype(BF16).reshape(4, 2, 2, 16, 1024)
-    for k in range(1, 4):
-        to, dev = along(2, k)
-        rcopy(sb.at[to], xg.at[c, y], y_s.at[k], y_r.at[k], dev).start()
-    xg[c, y] = sb[y]
-    rcopy(xg.at[c, y], xg.at[c, y], c_s.at[0], c_r.at[0], mate).start()
-    for k in range(1, 4):
-        come = lax.rem(y + 4 - k, 4)
-        rcopy(sb.at[come], xg.at[c, come], y_s.at[k], y_r.at[k], me).wait_recv()
-        rcopy(xg.at[c, come], xg.at[c, come], c_s.at[k], c_r.at[k], mate).start()
-    for k in range(4):
-        come = lax.rem(y + 4 - k, 4)
-        rcopy(xg.at[1 - c, come], xg.at[1 - c, come], c_s.at[k], c_r.at[k], mate).wait_recv()
-
+    def forward(cs, i):
+        at = pl.ds(lax.rem(x + 4 - i, 4) * 16, 16)
+        return rcopy(rg.at[cs, at], rg.at[cs, at], c_s.at[i], c_r.at[i], mate)
+
+    def widen(cs, i):
+        at = lax.rem(x + 4 - i, 4)
+        wide = rg[cs, pl.ds(at * 16, 16)].astype(F32).reshape(512, 128)
+        rf[cs, pl.ds(pl.multiple_of(at * 512, 512), 512)] = wide
+
+    for i in (0, 1, 3, 2):
+        scattered(sa, rg.at[c], a_s, a_r, i).wait_recv()
+        forward(c, i).start()
+        widen(c, i)
+    for i in (0, 1, 3, 2):
+        forward(1 - c, i).wait_recv()
+        widen(1 - c, i)
+        scattered(sa, rg.at[c], a_s, a_r, i).wait_send()
     for o in range(2):
-        xv[128 * o : 128 * o + 128] = xg[:, :, 0, o].reshape(128, 1024)
-        gv[128 * o : 128 * o + 128] = xg[:, :, 1, o].reshape(128, 1024)
+        for cs in range(2):
+            here = slice(128 * o + 64 * cs, 128 * o + 64 * cs + 64)
+            xv[here] = unfolded(rf.at[cs], 0, o).astype(BF16)
+            gv[here] = unfolded(rf.at[cs], 1, o).astype(BF16)
 
     for load in loads:
         load.wait()
@@ -307,43 +330,33 @@
     core = rcopy(part.at[:, :, 1 - c], rpart, q_s, q_r, mate)
     core.start()
     core.wait_recv()
+    mine = pl.multiple_of(64 * c, 64)
     for o in range(2):
-        layer = (part[0, o, c] + rpart[0, o]).astype(BF16)
-        grad = xg[c, :, 1, o].astype(F32) + (part[1, o, c] + rpart[1, o]).reshape(4, 16, 1024)
-        ret[:, 0, o] = layer.reshape(4, 16, 1024)
-        ret[:, 1, o] = grad.astype(BF16)
-    for k in range(1, 4):
-        to, dev = along(2, k)
-        rcopy(ret.at[to], ry.at[y], v_s.at[k], v_r.at[k], dev).start()
-    ry[y] = ret[y]
+        layer, grad = (part[i, o, c] + rpart[i, o] for i in range(2))
+        for j in range(8):
+            cols = slice(128 * j, 128 * j + 128)
+            own = gv[pl.ds(128 * o + mine, 64), cols].astype(F32)
+            sf[pl.ds(o * 8 + j, 64, stride=32), :] = layer[:, cols]
+            sf[pl.ds(16 + o * 8 + j, 64, stride=32), :] = own + grad[:, cols]
+    sa[...] = sf[...].reshape(64, 32, 128).astype(BF16)
+    scatter(sa, rz, z_s, z_r)
+    rz[chip] = sa[chip]
     add(0, 0)
     send(1, 0)
-    for k in range(1, 4):
-        come = lax.rem(y + 4 - k, 4)
-        rcopy(ret.at[come], ry.at[come], v_s.at[k], v_r.at[k], me).wait_recv()
-    unturn = jnp.where(r256 == swapped(l256), 1.0, 0.0).astype(BF16)
-    sz[...] = dot(unturn, ry[...].reshape(256, 1024)).astype(BF16).reshape(16, 16, 1024)
-
-    @pl.loop(1, 16)
-    def _(k):
-        to = lax.rem(xz + k, 16)
-        rcopy(sz.at[to], rz.at[xz], z_s.at[k], z_r.at[k], to * 8 + low).start()
-
-    rz[xz] = sz[xz]
     for block in range(1, 5):
         add(0, block)
         send(1, block)
 
-    @pl.loop(1, 16)
-    def _(k):
-        come = lax.rem(xz + 16 - k, 16)
-        rcopy(sz.at[come], rz.at[come], z_s.at[k], z_r.at[k], come * 8 + low).wait_recv()
-
-    got = rz[...].astype(F32)
-    unpick = jnp.where(srow[...] == rows, 1.0, 0.0).astype(BF16)
-    layer = dot(unpick, got[:, :8].reshape(128, 1024).astype(BF16))
+    for i in range(4):
+        scattered(sa, rz, z_s, z_r, i).wait_recv()
+    sf[...] = rz[...].astype(F32).reshape(2048, 128)
+    unpick = jnp.where(to_row(wanted) == rows.astype(F32), 1.0, 0.0).astype(BF16)
+    layer, grad = (
+        dot(unpick, jnp.concatenate([unfolded(sf, i, 0), unfolded(sf, i, 1)], axis=0).astype(BF16))
+        for i in range(2)
+    )
     out[...] = (tok[...].astype(F32) + layer).astype(BF16)
-    gx[...] = dot(unpick, got[:, 8:].reshape(128, 1024).astype(BF16)).astype(BF16)
+    gx[...] = grad.astype(BF16)
 
     for block in range(5):
         add(1, block)
@@ -376,28 +389,26 @@
         for f in range(4):
             gw1[:, pl.ds(f * 1024 + other + 128 * j, 128)] = rfin[4 + 4 * f + j]
 
-    @pl.loop(1, 16)
-    def _(k):
-        to = lax.rem(xz + k, 16)
-        rcopy(sa.at[to], ra.at[xz], a_s.at[k], a_r.at[k], to * 8 + low).wait_send()
-        rcopy(sz.at[to], rz.at[xz], z_s.at[k], z_r.at[k], to * 8 + low).wait_send()
+    for i in range(4):
+        scattered(sa, rz, z_s, z_r, i).wait_send()
 
     meta_copy.wait_send()
     stat_copy.wait_send()
     core.wait_send()
     last.wait_send()
-    for k in range(4):
-        come = lax.rem(y + 4 - k, 4)
-        rcopy(xg.at[c, come], xg.at[c, come], c_s.at[k], c_r.at[k], mate).wait_send()
+    for i in range(4):
+        forward(c, i).wait_send()
     for k in range(1, 4):
-        to, dev = along(2, k)
-        rcopy(sb.at[to], xg.at[c, y], y_s.at[k], y_r.at[k], dev).wait_send()
-        rcopy(ret.at[to], ry.at[y], v_s.at[k], v_r.at[k], dev).wait_send()
         for o in range(3):
             for block in range(5):
                 hop(0, block, o, k).wait_send()
                 hop(1, block, o, k).wait_send()
             hop(2, 0, o, k).wait_send()
+
+
+def hand_over(*refs):
+    for i in range(4):
+        refs[4 + i][...] = refs[i][...]
 
 
 def body(
@@ -411,8 +422,8 @@
         return pltpu.VMEM(shape, kind)
 
     scratch = [
-        v((4, 1024, 512)), v((1024, 512)), v((16, 16, 1024)), v((16, 16, 1024)),
-        v((4, 2, 2, 16, 1024)), v((2, 4, 2, 2, 16, 1024)), v((2, 8, 128), F32),
+        v((4, 1024, 512)), v((1024, 512)), v((2048, 128), F32), v((64, 32, 128)),
+        v((2, 64, 32, 128)), v((2, 2048, 128), F32), v((2, 8, 128), F32),
         v((8, 128, 128), F32), v((2, 128, 128), F32), v((256, 1024)), v((256, 1024)),
         v((1024, 256)), v((1024, 256)), v((4, 256, 512)), v((4, 256, 512), F32),
         v((8, 128, 128)), v((8, 128, 128), F32), v((256, 512), F32), v((256, 512), F32),
@@ -426,14 +437,12 @@
     scratch += [v((3, n, 16, 128)) for n in COUNT]
     scratch += [
         v((20, 16, 128), F32), v((20, 8, 128), F32), v((2, 2, 2, 64, 1024), F32),
-        v((2, 2, 64, 1024), F32), v((4, 2, 2, 16, 1024)), v((4, 2, 2, 16, 1024)),
-        v((16, 16, 1024)), v((16, 16, 1024)),
+        v((2, 2, 64, 1024), F32), v((64, 32, 128)),
     ]
-    scratch += [dma((5,)), dma((16,)), dma((16,)), dma((4,)), dma((4,)), dma((4,)), dma((4,))]
+    scratch += [dma((5,)), dma((4,)), dma((4,)), dma((4,)), dma((4,))]
     scratch += [dma, dma, dma, dma, dma((45,)), dma((45,)), dma((45,)), dma((45,))]
-    scratch += [dma((9,)), dma((9,)), dma, dma, dma, dma, dma((4,)), dma((4,)), dma((16,)), dma((16,))]
-    return tuple(
-        pl.pallas_call(
+    scratch += [dma((9,)), dma((9,)), dma, dma, dma, dma, dma((4,)), dma((4,))]
+    results = pl.pallas_call(
             kernel,
             out_shape=(
                 jax.ShapeDtypeStruct((128, 1024), BF16),
@@ -451,7 +460,12 @@
             tokens, grad_out, w_in, w_out, rel_bias, send_rows, recv_place, block_first,
             user_rows, stamps.reshape(1, 128),
         )
-    )
+    return pl.pallas_call(
+        hand_over,
+        out_shape=tuple(jax.ShapeDtypeStruct(r.shape, r.dtype) for r in results),
+        in_specs=[vmem] * 4,
+        out_specs=(vmem,) * 4,
+    )(*results)
 
 
 def solution(mesh):

time: 86.6 us -> 73.9 us (0.85)
  Pallas kernels: 78.1 us -> 71.8 us
  local copies, waits for them, and re-layouts: 6.28 us -> 0 us
    pallas_call x1, Pallas kernels: 78.1 us -> 69.9 us  [body(): pl.pallas_call(kernel, out_shape=(jax.ShapeDtypeStruct((128, 1024), BF16)...]
    unnamed x4 -> x0, local copies, waits for them, and re-layouts: 6.28 us -> none
    pallas_call x0 -> x1, Pallas kernels: none -> 1.92 us  [body(): pl.pallas_call(hand_over, out_shape=tuple((jax.ShapeDtypeStruct(r.shape,...]
where the time goes in v2:
time: 73.9 us; the launch traced here: 73.7 us
  Pallas kernels  71.8 us (97%)
  between operations  1.93 us (3%)
    pallas_call x1, Pallas kernels, body(): pl.pallas_call(kernel, out_shape=(jax.ShapeDtypeStruct((128, 1024), BF16)...  69.9 us
    pallas_call x1, Pallas kernels, body(): pl.pallas_call(hand_over, out_shape=tuple((jax.ShapeDtypeStruct(r.shape,...  1.92 us

profile of v2, /device:TPU:1, one launch (start us, length us, event | category | flops | bytes accessed | tf_op | source)
XLA Modules:
  0.0 73.7 jit_solution(5114027941776210089)
XLA Ops:
  1.9 69.9 %shard_map.129 = (bf16[128,1024]{1,0:T(8,128)(2,1)}, bf16[128,1024]{1,0:T(8,128)(2,1)}, f32[8,4096]{1,0:T(8,128)}, f32[8,1024]{1,0:T(8,128)}) custom-call(bf16[128,1024]{1,0:T(8,128)(2,1)} %tok.1, bf16[128,1024]{1,0:T(8,128)(2,1)} %gout.1, bf16[1024,4096]{1,0:T(8,128)(2,1)} %w_in.1, bf16[1024,1024]{1,0:T(8,128)(2,1)} %w_out.1, f32[8,16]{1,0:T(8,128)} %relb.1, ...), custom_call_target="tpu_custom_call" | custom-call | tf_op jit(solution)/shard_map/pallas_call | solution.py:445
  71.8 1.9 %shard_map.130 = (bf16[128,1024]{1,0:T(8,128)(2,1)}, bf16[128,1024]{1,0:T(8,128)(2,1)}, f32[8,4096]{1,0:T(8,128)}, f32[8,1024]{1,0:T(8,128)}) custom-call(bf16[128,1024]{1,0:T(8,128)(2,1)} %get-tuple-element.8.refs_0_, bf16[128,1024]{1,0:T(8,128)(2,1)} %get-tuple-element.9.refs_1_, f32[8,4096]{1,0:T(8,128)} %get-tuple-element.10.refs_2_, ...), custom_call_target="tpu_custom_call" | custom-call | tf_op jit(solution)/shard_map/pallas_call | solution.py:463

commit v3 on v2

--- a/solution.py
+++ b/solution.py
@@ -24,15 +24,16 @@
 
 
 def kernel(
-    tok, gout, w_in, w_out, relb, srow, rplace, first, live, stamps,
+    tok_in, gout_in, w_in, w_out, relb_in, srow_in, rplace_in, first, live, stamps_in,
     out, gx, gw1, gw2,
-    wi, wo, sf, sa, rg, rf, meta, bias, mask, xv, gv, xt, gt, act, slp, pw, ps, mix, gg,
-    stat, ga, gm, gp, b0, b1, b2, r10, r11, r12, s10, s11, s12, r20, r21, r22, s20, s21, s22,
+    tok, gout, relb, srow, rplace, stamps, wi, wo, sf, sa, rg, rf, meta, bias, mask, xv, gv, xt, gt, act, slp, pw, ps, mix, gg,
+    stat, ga, gm, gp, b0, b1, b2, r10, r11, r12, h0, h1, h2, n0, n1, n2, s10, s11, s12, r20, r21, r22, s20, s21, s22,
     r30, r31, r32, fin, rfin, part, rpart, rz,
-    wsem, a_s, a_r, c_s, c_r, m_s, m_r, t_s, t_r, p1_s, p1_r, p2_s, p2_r, p3_s, p3_r,
+    in_sem, wsem, a_s, a_r, c_s, c_r, m_s, m_r, t_s, t_r, p1_s, p1_r, p2_s, p2_r, p3_s, p3_r,
     f_s, f_r, q_s, q_r, z_s, z_r,
 ):
     bs, r1, s1, r2 = (b0, b1, b2), (r10, r11, r12), (s10, s11, s12), (r20, r21, r22)
+    halves, nears = (h0, h1, h2), (n0, n1, n2)
     s2, r3 = (s20, s21, s22), (r30, r31, r32)
     me = lax.axis_index("seq")
     c = lax.rem(me, 2)
@@ -53,15 +54,24 @@
             device_id=(dev,), device_id_type=MESH,
         )
 
+    inputs = [
+        pltpu.make_async_copy(src, dst, in_sem.at[i])
+        for i, (src, dst) in enumerate(
+            ((srow_in, srow), (tok_in, tok), (gout_in, gout), (rplace_in, rplace),
+             (stamps_in, stamps), (relb_in, relb))
+        )
+    ]
+    for load in inputs:
+        load.start()
     barrier = pltpu.get_barrier_semaphore()
+
+    pl.semaphore_signal(barrier, inc=1, device_id=(mate,), device_id_type=MESH)
 
     @pl.loop(1, 64)
     def _(k):
         pl.semaphore_signal(
             barrier, inc=1, device_id=(lax.rem(chip + k, 64) * 2 + c,), device_id_type=MESH
         )
-
-    pl.semaphore_signal(barrier, inc=1, device_id=(mate,), device_id_type=MESH)
 
     half = pl.multiple_of(c * 512, 512)
     loads = [
@@ -69,8 +79,6 @@
         for f in range(4)
     ]
     loads.append(pltpu.make_async_copy(w_out.at[:, pl.ds(half, 512)], wo, wsem.at[4]))
-    for load in loads:
-        load.start()
 
     rows = lax.broadcasted_iota(jnp.int32, (128, 128), 0)
     lanes = lax.broadcasted_iota(jnp.int32, (128, 128), 1)
@@ -82,27 +90,29 @@
     def to_row(column):
         return jnp.sum(jnp.where(eye, column, 0.0), axis=0, keepdims=True)
 
+    for load in inputs:
+        load.wait()
     order = ((rows & 63) << 1) + (rows >> 6)
     wanted = jnp.sum(
         jnp.where(lanes == order, srow[...].astype(F32), 0.0), axis=1, keepdims=True
     )
     pick = jnp.where(wanted == lanes.astype(F32), 1.0, 0.0).astype(BF16)
 
-    def fold(value, kind):
+    def fold(value, kind, start=0):
         for o in range(2):
             for j in range(8):
-                sf[pl.ds(kind * 16 + o * 8 + j, 64, stride=32), :] = value[
-                    64 * o : 64 * o + 64, 128 * j : 128 * j + 128
-                ]
-
-    def unfolded(ref, kind, o):
+                sf[kind, pl.ds(o * 8 + j, 64, stride=16), :] = value(
+                    slice(64 * o, 64 * o + 64), slice(128 * j, 128 * j + 128)
+                )
+        sa[:, 16 * kind : 16 * kind + 16] = sf[kind].reshape(64, 16, 128).astype(BF16)
+
+    def unfolded(ref, o):
         return jnp.concatenate(
-            [ref[pl.ds(kind * 16 + o * 8 + j, 64, stride=32), :] for j in range(8)], axis=1
-        )
-
-    fold(dot(pick, tok[...]), 0)
-    fold(dot(pick, gout[...]), 1)
-    sa[...] = sf[...].reshape(64, 32, 128).astype(BF16)
+            [ref[pl.ds(o * 8 + j, 64, stride=16), :] for j in range(8)], axis=1
+        ).astype(BF16)
+
+    picked = dot(pick, tok[...])
+    fold(lambda at, cols: picked[at, cols], 0)
 
     pl.semaphore_wait(barrier, 64)
 
@@ -110,27 +120,40 @@
         there = lax.rem(x + i, 4) * 16 + lax.rem(z * 4 + y + j, 16)
         return there, there * 2 + c
 
-    def scatter(src, dst, sends, recvs):
+    def scatter(rows, dst, sends, recvs):
         @pl.loop(0, 16)
         def _(j):
             for i in range(4):
                 there, dev = peer(i, j)
 
                 def go():
-                    rcopy(src.at[there], dst.at[chip], sends.at[i], recvs.at[i], dev).start()
+                    src = sa.at[there, rows]
+                    rcopy(src, dst.at[chip], sends.at[i], recvs.at[i], dev).start()
 
                 if i == 0:
                     pl.when(j > 0)(go)
                 else:
                     go()
 
-    def scattered(src, dst, sends, recvs, i):
-        come = lax.rem(x + 4 - i, 4) * 16
-        at = pl.ds(come, 16 if i else 15)
-        return rcopy(src.at[at], dst.at[at], sends.at[i], recvs.at[i], mate)
-
-    scatter(sa, rg.at[c], a_s, a_r)
-    rg[c, chip] = sa[chip]
+    def scattered(dst, sends, recvs, i):
+        ref = dst.at[pl.ds(lax.rem(x + 4 - i, 4) * 16, 16 if i else 15)]
+        return rcopy(ref, ref, sends.at[i], recvs.at[i], mate)
+
+    def outward(kind, i):
+        at = pl.ds(4 * kind, 4)
+        return scattered(rg.at[kind, c], a_s.at[at], a_r.at[at], i)
+
+    def leave(kind):
+        rows, at = pl.ds(16 * kind, 16), pl.ds(4 * kind, 4)
+        scatter(rows, rg.at[kind, c], a_s.at[at], a_r.at[at])
+        rg[kind, c, chip] = sa[chip, rows]
+
+    leave(0)
+    picked_g = dot(pick, gout[...])
+    fold(lambda at, cols: picked_g[at, cols], 1)
+    leave(1)
+    for load in loads:
+        load.start()
 
     m = rplace[...]
     place = (m & 1) * 64 + (m >> 1)
@@ -163,38 +186,47 @@
                 value = jnp.where(spread >= float(2**k), relb[4 * c + h, k + 1], value)
             bias[4 * o + h] = value
 
-    def forward(cs, i):
+    def forward(kind, cs, i):
         at = pl.ds(lax.rem(x + 4 - i, 4) * 16, 16)
-        return rcopy(rg.at[cs, at], rg.at[cs, at], c_s.at[i], c_r.at[i], mate)
-
-    def widen(cs, i):
+        ref = rg.at[kind, cs, at]
+        return rcopy(ref, ref, c_s.at[4 * kind + i], c_r.at[4 * kind + i], mate)
+
+    def widen(kind, cs, i):
         at = lax.rem(x + 4 - i, 4)
-        wide = rg[cs, pl.ds(at * 16, 16)].astype(F32).reshape(512, 128)
-        rf[cs, pl.ds(pl.multiple_of(at * 512, 512), 512)] = wide
-
-    for i in (0, 1, 3, 2):
-        scattered(sa, rg.at[c], a_s, a_r, i).wait_recv()
-        forward(c, i).start()
-        widen(c, i)
-    for i in (0, 1, 3, 2):
-        forward(1 - c, i).wait_recv()
-        widen(1 - c, i)
-        scattered(sa, rg.at[c], a_s, a_r, i).wait_send()
-    for o in range(2):
-        for cs in range(2):
-            here = slice(128 * o + 64 * cs, 128 * o + 64 * cs + 64)
-            xv[here] = unfolded(rf.at[cs], 0, o).astype(BF16)
-            gv[here] = unfolded(rf.at[cs], 1, o).astype(BF16)
-
+        wide = rg[kind, cs, pl.ds(at * 16, 16)].astype(F32).reshape(256, 128)
+        rf[kind, cs, pl.ds(pl.multiple_of(at * 256, 256), 256)] = wide
+
+    def arrive(kind):
+        for i in (0, 1, 3, 2):
+            outward(kind, i).wait_recv()
+            forward(kind, c, i).start()
+            widen(kind, c, i)
+
+    def complete(kind, into):
+        for i in (0, 1, 3, 2):
+            forward(kind, 1 - c, i).wait_recv()
+            widen(kind, 1 - c, i)
+        for o in range(2):
+            for cs in range(2):
+                here = slice(128 * o + 64 * cs, 128 * o + 64 * cs + 64)
+                into[here] = unfolded(rf.at[kind, cs], o)
+
+    arrive(0)
+    complete(0, xv)
     for load in loads:
         load.wait()
 
-    for f in range(4):
+    def project(f):
         pre = dot(xv[...], wi[f])
         sig = jax.nn.sigmoid(pre)
         act[f] = (pre * sig).astype(BF16)
         slp[f] = sig * (1.0 + pre * (1.0 - sig))
-    gg[...] = dot(gv[...], wo[...])
+
+    project(1)
+    project(2)
+    arrive(1)
+    project(3)
+    project(0)
     heads = [(o, h) for o in range(2) for h in range(4)]
     scale = 128**-0.5
     for o, h in heads:
@@ -207,6 +239,9 @@
         pw[4 * o + h] = w
         ps[4 * o + h] = jnp.where(allowed, sig * (1.0 + logits * (1.0 - sig)), 0.0)
         mix[here] = dot(w, v)
+
+    complete(1, gv)
+    gg[...] = dot(gv[...], wo[...])
 
     gn = gg[...] * act[0].astype(F32)
     mixed = mix[...]
@@ -240,7 +275,7 @@
     gp[0] = ((ggv * normed).astype(BF16).astype(F32) * slp[0]).astype(BF16)
 
     def product(block, left, right):
-        @pl.loop(0, 4)
+        @pl.loop(0, 4, unroll=True)
         def _(i):
             rows = pl.ds(pl.multiple_of(i * 256, 256), 256)
             tile = dot(left[rows, :], right).astype(BF16)
@@ -258,49 +293,90 @@
                     for k in range(4):
                         bs[2][at, :, i, k] = part4[k]
 
+    def tiles(block):
+        return [(o, t) for o in range(3) for t in range(slots(block, o)[0], sum(slots(block, o)))]
+
+    def near(step, o, t):
+        here = coords[o]
+        turn = 1 - 2 * lax.rem(here + t + c, 2)
+        one, two = lax.rem(here + 4 + turn, 4), lax.rem(here + 4 - turn, 4)
+        i = (sum(COUNT[:o]) + t) * 3
+        sems = [(p1_s.at[i + n], p1_r.at[i + n]) for n in range(3)]
+        if step == 0:
+            dev = me + (one - here) * strides[o]
+            return [
+                rcopy(bs[o].at[t, quarter], r1[o].at[t, n], *sems[n], dev)
+                for n, quarter in ((1, lax.rem(here + 2, 4)), (0, one))
+            ]
+        return two, rcopy(halves[o].at[t], nears[o].at[t], *sems[2], me + (two - here) * strides[o])
+
+    def near_send(block):
+        for o, t in tiles(block):
+            for copy in near(0, o, t):
+                copy.start()
+
+    def near_pass(block):
+        for o, t in tiles(block):
+            near(0, o, t)[0].wait_recv()
+            two, copy = near(1, o, t)
+            halves[o][t] = (bs[o][t, two].astype(F32) + r1[o][t, 1].astype(F32)).astype(BF16)
+            copy.start()
+
+    def near_add(block):
+        for o, t in tiles(block):
+            near(0, o, t)[1].wait_recv()
+            near(1, o, t)[1].wait_recv()
+            value = bs[o][t, coords[o]].astype(F32) + r1[o][t, 0].astype(F32)
+            s1[o][t] = (value + nears[o][t].astype(F32)).astype(BF16)
+
     def hop(stage, block, o, k):
-        axis = (o + stage) % 3
-        there, dev = along(axis, k)
-        if stage < 2:
+        there, dev = along((o + stage) % 3, k)
+        if stage == 1:
             start, count = slots(block, o)
             at = pl.ds(start, count)
             i = (block * 3 + o) * 3 + k - 1
-            src, dst = ((bs, r1), (s1, r2))[stage]
-            send, recv = ((p1_s, p1_r), (p2_s, p2_r))[stage]
-            return rcopy(
-                src[o].at[at, there], dst[o].at[k - 1, at], send.at[i], recv.at[i], dev
-            )
+            return rcopy(s1[o].at[at, there], r2[o].at[k - 1, at], p2_s.at[i], p2_r.at[i], dev)
         i = o * 3 + k - 1
         return rcopy(s2[o].at[:, there], r3[o].at[k - 1], p3_s.at[i], p3_r.at[i], dev)
 
-    def send(stage, block):
+    def far_send(block):
+        near_add(block)
         for k in (2, 1, 3):
             for o in range(3):
-                hop(stage, block, o, k).start()
-
-    def add(stage, block):
+                hop(1, block, o, k).start()
+
+    def far_add(block):
         for o in range(3):
             for k in range(1, 4):
-                hop(stage, block, o, k).wait_recv()
-            here = coords[(o + stage) % 3]
+                hop(1, block, o, k).wait_recv()
             start, count = slots(block, o)
             at = slice(start, start + count)
-            if stage == 0:
-                value = bs[o][at, here].astype(F32)
-                for k in range(3):
-                    value = value + r1[o][k, at].astype(F32)
-                s1[o][at] = value.astype(BF16)
-            else:
-                value = s1[o][at, here].astype(F32)
-                for k in range(3):
-                    value = value + r2[o][k, at].astype(F32)
-                s2[o][at] = value.astype(BF16)
+            value = s1[o][at, coords[(o + 1) % 3]].astype(F32)
+            for k in range(3):
+                value = value + r2[o][k, at].astype(F32)
+            s2[o][at] = value.astype(BF16)
 
     product(0, gt, ga[...])
-    send(0, 0)
+    near_send(0)
     product(1, xt, gp[0])
-    send(0, 1)
+    near_send(1)
     part[0] = dot(ga[...], wo[...], ((1,), (1,))).reshape(2, 2, 64, 1024)
+
+    def across(kind):
+        return rcopy(part.at[kind, :, 1 - c], rpart.at[kind], q_s.at[kind], q_r.at[kind], mate)
+
+    def home(kind):
+        across(kind).wait_recv()
+        mine = pl.multiple_of(64 * c, 64)
+        total = [part[kind, o, c] + rpart[kind, o] for o in range(2)]
+        if kind:
+            for o in range(2):
+                total[o] = total[o] + gv[pl.ds(128 * o + mine, 64), :].astype(F32)
+        for i in range(4):
+            outward(kind, i).wait_send()
+        fold(lambda at, cols: total[at.start // 64][:, cols], kind)
+
+    across(0).start()
 
     for o, h in heads:
         here = (slice(128 * o, 128 * o + 128), slice(128 * h, 128 * h + 128))
@@ -318,51 +394,46 @@
             ).astype(BF16)
 
     product(2, xt, gp[1])
-    send(0, 2)
+    near_send(2)
+    near_pass(0)
     product(3, xt, gp[2])
-    send(0, 3)
+    near_send(3)
+    near_pass(1)
     product(4, xt, gp[3])
-    send(0, 4)
+    near_send(4)
     back = dot(gp[0], wi[0], ((1,), (1,)))
     for f in range(1, 4):
         back = back + dot(gp[f], wi[f], ((1,), (1,)))
     part[1] = back.reshape(2, 2, 64, 1024)
-    core = rcopy(part.at[:, :, 1 - c], rpart, q_s, q_r, mate)
-    core.start()
-    core.wait_recv()
-    mine = pl.multiple_of(64 * c, 64)
-    for o in range(2):
-        layer, grad = (part[i, o, c] + rpart[i, o] for i in range(2))
-        for j in range(8):
-            cols = slice(128 * j, 128 * j + 128)
-            own = gv[pl.ds(128 * o + mine, 64), cols].astype(F32)
-            sf[pl.ds(o * 8 + j, 64, stride=32), :] = layer[:, cols]
-            sf[pl.ds(16 + o * 8 + j, 64, stride=32), :] = own + grad[:, cols]
-    sa[...] = sf[...].reshape(64, 32, 128).astype(BF16)
-    scatter(sa, rz, z_s, z_r)
+    across(1).start()
+    near_pass(2)
+    home(0)
+    near_pass(3)
+    home(1)
+    near_pass(4)
+    for block in range(5):
+        far_send(block)
+    scatter(pl.ds(0, 32), rz, z_s, z_r)
     rz[chip] = sa[chip]
-    add(0, 0)
-    send(1, 0)
-    for block in range(1, 5):
-        add(0, block)
-        send(1, block)
-
-    for i in range(4):
-        scattered(sa, rz, z_s, z_r, i).wait_recv()
-    sf[...] = rz[...].astype(F32).reshape(2048, 128)
-    unpick = jnp.where(to_row(wanted) == rows.astype(F32), 1.0, 0.0).astype(BF16)
-    layer, grad = (
-        dot(unpick, jnp.concatenate([unfolded(sf, i, 0), unfolded(sf, i, 1)], axis=0).astype(BF16))
-        for i in range(2)
-    )
-    out[...] = (tok[...].astype(F32) + layer).astype(BF16)
-    gx[...] = grad.astype(BF16)
-
     for block in range(5):
-        add(1, block)
+        far_add(block)
     for k in (2, 1, 3):
         for o in range(3):
             hop(2, 0, o, k).start()
+    unpick = jnp.where(to_row(wanted) == rows.astype(F32), 1.0, 0.0).astype(BF16)
+
+    for i in range(4):
+        scattered(rz, z_s, z_r, i).wait_recv()
+
+    def returned(kind):
+        sf[kind] = rz[:, 16 * kind : 16 * kind + 16].astype(F32).reshape(1024, 128)
+        return dot(
+            unpick, jnp.concatenate([unfolded(sf.at[kind], o) for o in range(2)], axis=0)
+        )
+
+    out[...] = (tok[...].astype(F32) + returned(0)).astype(BF16)
+    gx[...] = returned(1).astype(BF16)
+
     for o in range(3):
         for k in range(1, 4):
             hop(2, 0, o, k).wait_recv()
@@ -390,20 +461,23 @@
             gw1[:, pl.ds(f * 1024 + other + 128 * j, 128)] = rfin[4 + 4 * f + j]
 
     for i in range(4):
-        scattered(sa, rz, z_s, z_r, i).wait_send()
-
+        scattered(rz, z_s, z_r, i).wait_send()
+        for kind in range(2):
+            forward(kind, c, i).wait_send()
+    for kind in range(2):
+        across(kind).wait_send()
     meta_copy.wait_send()
     stat_copy.wait_send()
-    core.wait_send()
     last.wait_send()
-    for i in range(4):
-        forward(c, i).wait_send()
     for k in range(1, 4):
         for o in range(3):
             for block in range(5):
-                hop(0, block, o, k).wait_send()
                 hop(1, block, o, k).wait_send()
             hop(2, 0, o, k).wait_send()
+    for block in range(5):
+        for o, t in tiles(block):
+            for copy in near(0, o, t) + [near(1, o, t)[1]]:
+                copy.wait_send()
 
 
 def hand_over(*refs):
@@ -422,15 +496,19 @@
         return pltpu.VMEM(shape, kind)
 
     scratch = [
-        v((4, 1024, 512)), v((1024, 512)), v((2048, 128), F32), v((64, 32, 128)),
-        v((2, 64, 32, 128)), v((2, 2048, 128), F32), v((2, 8, 128), F32),
+        v((128, 1024)), v((128, 1024)), pltpu.SMEM((8, 16), F32), v((1, 128), jnp.int32),
+        v((1, 128), jnp.int32), v((1, 128), jnp.int32),
+        v((4, 1024, 512)), v((1024, 512)), v((2, 1024, 128), F32), v((64, 32, 128)),
+        v((2, 2, 64, 16, 128)), v((2, 2, 1024, 128), F32), v((2, 8, 128), F32),
         v((8, 128, 128), F32), v((2, 128, 128), F32), v((256, 1024)), v((256, 1024)),
         v((1024, 256)), v((1024, 256)), v((4, 256, 512)), v((4, 256, 512), F32),
         v((8, 128, 128)), v((8, 128, 128), F32), v((256, 512), F32), v((256, 512), F32),
         v((2, 256, 128), F32), v((256, 512)), v((256, 512)), v((4, 256, 512)),
     ]
     scratch += [v((n, 4, 4, 4, 16, 128)) for n in COUNT]
-    scratch += [v((3, n, 4, 4, 16, 128)) for n in COUNT]
+    scratch += [v((n, 2, 4, 4, 16, 128)) for n in COUNT]
+    scratch += [v((n, 4, 4, 16, 128)) for n in COUNT]
+    scratch += [v((n, 4, 4, 16, 128)) for n in COUNT]
     scratch += [v((n, 4, 4, 16, 128)) for n in COUNT]
     scratch += [v((3, n, 4, 16, 128)) for n in COUNT]
     scratch += [v((n, 4, 16, 128)) for n in COUNT]
@@ -439,9 +517,9 @@
         v((20, 16, 128), F32), v((20, 8, 128), F32), v((2, 2, 2, 64, 1024), F32),
         v((2, 2, 64, 1024), F32), v((64, 32, 128)),
     ]
-    scratch += [dma((5,)), dma((4,)), dma((4,)), dma((4,)), dma((4,))]
-    scratch += [dma, dma, dma, dma, dma((45,)), dma((45,)), dma((45,)), dma((45,))]
-    scratch += [dma((9,)), dma((9,)), dma, dma, dma, dma, dma((4,)), dma((4,))]
+    scratch += [dma((6,)), dma((5,)), dma((8,)), dma((8,)), dma((8,)), dma((8,))]
+    scratch += [dma, dma, dma, dma, dma((60,)), dma((60,)), dma((45,)), dma((45,))]
+    scratch += [dma((9,)), dma((9,)), dma, dma, dma((2,)), dma((2,)), dma((4,)), dma((4,))]
     results = pl.pallas_call(
             kernel,
             out_shape=(
@@ -450,7 +528,7 @@
                 jax.ShapeDtypeStruct((8, 4096), F32),
                 jax.ShapeDtypeStruct((8, 1024), F32),
             ),
-            in_specs=[vmem, vmem, hbm, hbm, smem, vmem, vmem, smem, smem, vmem],
+            in_specs=[hbm] * 7 + [smem, smem, hbm],
             out_specs=(vmem, vmem, vmem, vmem),
             scratch_shapes=scratch,
             compiler_params=pltpu.CompilerParams(

time: 73.9 us -> 65.5 us (0.89)
  Pallas kernels: 71.8 us -> 63.4 us
    pallas_call x1, Pallas kernels: 69.9 us -> 61.5 us  [body(): pl.pallas_call(kernel, out_shape=(jax.ShapeDtypeStruct((128, 1024), BF16)...]
where the time goes in v3:
time: 65.5 us; the launch traced here: 65.4 us
  Pallas kernels  63.4 us (97%)
  between operations  1.93 us (3%)
    pallas_call x1, Pallas kernels, body(): pl.pallas_call(kernel, out_shape=(jax.ShapeDtypeStruct((128, 1024), BF16)...  61.5 us
    pallas_call x1, Pallas kernels, body(): pl.pallas_call(hand_over, out_shape=tuple((jax.ShapeDtypeStruct(r.shape,...  1.92 us

profile of v3, /device:TPU:1, one launch (start us, length us, event | category | flops | bytes accessed | tf_op | source)
XLA Modules:
  0.0 65.4 jit_solution(183182085370614137)
XLA Ops:
  1.9 61.5 %shard_map.129 = (bf16[128,1024]{1,0:T(8,128)(2,1)}, bf16[128,1024]{1,0:T(8,128)(2,1)}, f32[8,4096]{1,0:T(8,128)}, f32[8,1024]{1,0:T(8,128)}) custom-call(bf16[128,1024]{1,0:T(8,128)(2,1)} %tok_in.1, bf16[128,1024]{1,0:T(8,128)(2,1)} %gout_in.1, bf16[1024,4096]{1,0:T(8,128)(2,1)} %w_in.1, bf16[1024,1024]{1,0:T(8,128)(2,1)} %w_out.1, f32[8,16]{1,0:T(8,128)} %relb_in.1, ...), custom_call_target="tpu_custom_call" | custom-call | tf_op jit(solution)/shard_map/pallas_call | solution.py:523
  63.4 1.9 %shard_map.130 = (bf16[128,1024]{1,0:T(8,128)(2,1)}, bf16[128,1024]{1,0:T(8,128)(2,1)}, f32[8,4096]{1,0:T(8,128)}, f32[8,1024]{1,0:T(8,128)}) custom-call(bf16[128,1024]{1,0:T(8,128)(2,1)} %get-tuple-element.8.refs_0_, bf16[128,1024]{1,0:T(8,128)(2,1)} %get-tuple-element.9.refs_1_, f32[8,4096]{1,0:T(8,128)} %get-tuple-element.10.refs_2_, ...), custom_call_target="tpu_custom_call" | custom-call | tf_op jit(solution)/shard_map/pallas_call | solution.py:541

commit v4 on v3

--- a/solution.py
+++ b/solution.py
@@ -28,9 +28,9 @@
     out, gx, gw1, gw2,
     tok, gout, relb, srow, rplace, stamps, wi, wo, sf, sa, rg, rf, meta, bias, mask, xv, gv, xt, gt, act, slp, pw, ps, mix, gg,
     stat, ga, gm, gp, b0, b1, b2, r10, r11, r12, h0, h1, h2, n0, n1, n2, s10, s11, s12, r20, r21, r22, s20, s21, s22,
-    r30, r31, r32, fin, rfin, part, rpart, rz,
+    r30, r31, r32, fin, rfin, part, rpart, rz, xn, yn,
     in_sem, wsem, a_s, a_r, c_s, c_r, m_s, m_r, t_s, t_r, p1_s, p1_r, p2_s, p2_r, p3_s, p3_r,
-    f_s, f_r, q_s, q_r, z_s, z_r,
+    f_s, f_r, q_s, q_r, z_s, z_r, e_s, e_r,
 ):
     bs, r1, s1, r2 = (b0, b1, b2), (r10, r11, r12), (s10, s11, s12), (r20, r21, r22)
     halves, nears = (h0, h1, h2), (n0, n1, n2)
@@ -213,6 +213,30 @@
 
     arrive(0)
     complete(0, xv)
+
+    def pair(o, e):
+        here = coords[o]
+        turn = 1 - 2 * lax.rem(here + e + c, 2)
+        one, two = lax.rem(here + 4 + turn, 4), lax.rem(here + 4 - turn, 4)
+        to_one, to_two = (me + (n - here) * strides[o] for n in (one, two))
+        return here, lax.rem(here + 2, 4), one, two, to_one, to_two
+
+    def quarter(ref, o, q):
+        return ref.at[(slice(None),) * o + (q,)]
+
+    def early(o, e):
+        _, across, one, _, dev, _ = pair(o, e)
+        i = (o * 2 + e) * 2
+        return [
+            rcopy(quarter(xt, o, q), xn.at[o, e, n], e_s.at[i + n], e_r.at[i + n], dev)
+            for n, q in ((1, across), (0, one))
+        ]
+
+    xt[...] = xv[...].T.reshape(4, 4, 4, 16, 256)
+    for e in range(2):
+        for o in range(3):
+            for copy in early(o, e):
+                copy.start()
     for load in loads:
         load.wait()
 
@@ -256,8 +280,7 @@
     )
     stat_copy = rcopy(stat.at[c], stat.at[c], t_s, t_r, mate)
     stat_copy.start()
-    xt[...] = xv[...].T
-    gt[...] = gv[...].T
+    gt[...] = gv[...].T.reshape(4, 4, 4, 16, 256)
     rcopy(stat.at[1 - c], stat.at[1 - c], t_s, t_r, mate).wait_recv()
     theirs = stat[1 - c]
     total2, square2, gsum2, gdot2 = (theirs[:, i : i + 1] for i in range(4))
@@ -277,8 +300,7 @@
     def product(block, left, right):
         @pl.loop(0, 4, unroll=True)
         def _(i):
-            rows = pl.ds(pl.multiple_of(i * 256, 256), 256)
-            tile = dot(left[rows, :], right).astype(BF16)
+            tile = dot(left[i].reshape(256, 256), right).astype(BF16)
             seen = [0, 0, 0]
             for j in range(4):
                 o = ORDERS[block][j]
@@ -297,37 +319,66 @@
         return [(o, t) for o in range(3) for t in range(slots(block, o)[0], sum(slots(block, o)))]
 
     def near(step, o, t):
-        here = coords[o]
-        turn = 1 - 2 * lax.rem(here + t + c, 2)
-        one, two = lax.rem(here + 4 + turn, 4), lax.rem(here + 4 - turn, 4)
+        _, across, one, two, dev, dev2 = pair(o, t % 2)
         i = (sum(COUNT[:o]) + t) * 3
         sems = [(p1_s.at[i + n], p1_r.at[i + n]) for n in range(3)]
         if step == 0:
-            dev = me + (one - here) * strides[o]
             return [
-                rcopy(bs[o].at[t, quarter], r1[o].at[t, n], *sems[n], dev)
-                for n, quarter in ((1, lax.rem(here + 2, 4)), (0, one))
+                rcopy(bs[o].at[t, q], r1[o].at[t, n], *sems[n], dev)
+                for n, q in ((1, across), (0, one))
             ]
-        return two, rcopy(halves[o].at[t], nears[o].at[t], *sems[2], me + (two - here) * strides[o])
+        return two, rcopy(halves[o].at[t], nears[o].at[t], *sems[2], dev2)
+
+    def swap(block, o, t):
+        j = [j for j in range(4) if ORDERS[block][j] == o][t - slots(block, o)[0]]
+        i = sum(COUNT[:o]) + t
+        mine, theirs = gp.at[block - 1, :, pl.ds(128 * j, 128)], yn.at[i]
+        return mine, theirs, rcopy(mine, theirs, p1_s.at[3 * i], p1_r.at[3 * i], pair(o, t % 2)[4])
 
     def near_send(block):
         for o, t in tiles(block):
-            for copy in near(0, o, t):
+            for copy in near(0, o, t) if block < 2 else [swap(block, o, t)[2]]:
                 copy.start()
+
+    came = set()
 
     def near_pass(block):
         for o, t in tiles(block):
-            near(0, o, t)[0].wait_recv()
-            two, copy = near(1, o, t)
-            halves[o][t] = (bs[o][t, two].astype(F32) + r1[o][t, 1].astype(F32)).astype(BF16)
-            copy.start()
+            e = t % 2
+            here, _, _, two, _, _ = pair(o, e)
+            copy = near(1, o, t)[1]
+            if block < 2:
+                near(0, o, t)[0].wait_recv()
+                halves[o][t] = (bs[o][t, two].astype(F32) + r1[o][t, 1].astype(F32)).astype(BF16)
+                copy.start()
+                continue
+            if (o, e) not in came:
+                came.add((o, e))
+                for arrival in early(o, e):
+                    arrival.wait_recv()
+            mine, theirs, swapped = swap(block, o, t)
+            swapped.wait_recv()
+            for n, q in ((1, two), (0, here)):
+                left = quarter(xt, o, q)[...].reshape(256, 256)
+                value = dot(left, mine[...]) + dot(xn[o, e, n].reshape(256, 256), theirs[...])
+                value = value.astype(BF16).reshape(4, 4, 16, 128)
+                into = halves[o].at[t] if n else bs[o].at[t, here]
+                if o == 1:
+                    for k in range(4):
+                        into[:, k] = value[k]
+                else:
+                    into[...] = value
+                if n:
+                    copy.start()
 
     def near_add(block):
         for o, t in tiles(block):
-            near(0, o, t)[1].wait_recv()
             near(1, o, t)[1].wait_recv()
-            value = bs[o][t, coords[o]].astype(F32) + r1[o][t, 0].astype(F32)
-            s1[o][t] = (value + nears[o][t].astype(F32)).astype(BF16)
+            value = bs[o][t, coords[o]].astype(F32) + nears[o][t].astype(F32)
+            if block < 2:
+                near(0, o, t)[1].wait_recv()
+                value = value + r1[o][t, 0].astype(F32)
+            s1[o][t] = value.astype(BF16)
 
     def hop(stage, block, o, k):
         there, dev = along((o + stage) % 3, k)
@@ -393,25 +444,23 @@
                 grads[f - 1].astype(BF16).astype(F32) * slp[(f,) + here]
             ).astype(BF16)
 
-    product(2, xt, gp[1])
-    near_send(2)
+    for block in range(2, 5):
+        near_send(block)
     near_pass(0)
-    product(3, xt, gp[2])
-    near_send(3)
     near_pass(1)
-    product(4, xt, gp[3])
-    near_send(4)
     back = dot(gp[0], wi[0], ((1,), (1,)))
     for f in range(1, 4):
         back = back + dot(gp[f], wi[f], ((1,), (1,)))
     part[1] = back.reshape(2, 2, 64, 1024)
     across(1).start()
     near_pass(2)
+    near_pass(3)
+    near_pass(4)
+    far_send(0)
+    far_send(1)
     home(0)
-    near_pass(3)
     home(1)
-    near_pass(4)
-    for block in range(5):
+    for block in range(2, 5):
         far_send(block)
     scatter(pl.ds(0, 32), rz, z_s, z_r)
     rz[chip] = sa[chip]
@@ -420,20 +469,6 @@
     for k in (2, 1, 3):
         for o in range(3):
             hop(2, 0, o, k).start()
-    unpick = jnp.where(to_row(wanted) == rows.astype(F32), 1.0, 0.0).astype(BF16)
-
-    for i in range(4):
-        scattered(rz, z_s, z_r, i).wait_recv()
-
-    def returned(kind):
-        sf[kind] = rz[:, 16 * kind : 16 * kind + 16].astype(F32).reshape(1024, 128)
-        return dot(
-            unpick, jnp.concatenate([unfolded(sf.at[kind], o) for o in range(2)], axis=0)
-        )
-
-    out[...] = (tok[...].astype(F32) + returned(0)).astype(BF16)
-    gx[...] = returned(1).astype(BF16)
-
     for o in range(3):
         for k in range(1, 4):
             hop(2, 0, o, k).wait_recv()
@@ -448,6 +483,20 @@
     away, home = pl.multiple_of(8 * (1 - c), 8), pl.multiple_of(8 * c, 8)
     last = rcopy(fin.at[:, pl.ds(away, 8)], rfin, f_s, f_r, mate)
     last.start()
+    unpick = jnp.where(to_row(wanted) == rows.astype(F32), 1.0, 0.0).astype(BF16)
+
+    for i in range(4):
+        scattered(rz, z_s, z_r, i).wait_recv()
+
+    def returned(kind):
+        sf[kind] = rz[:, 16 * kind : 16 * kind + 16].astype(F32).reshape(1024, 128)
+        return dot(
+            unpick, jnp.concatenate([unfolded(sf.at[kind], o) for o in range(2)], axis=0)
+        )
+
+    out[...] = (tok[...].astype(F32) + returned(0)).astype(BF16)
+    gx[...] = returned(1).astype(BF16)
+
     other = pl.multiple_of(512 - half, 512)
     mine = fin[:, pl.ds(home, 8)]
     for j in range(4):
@@ -476,7 +525,12 @@
             hop(2, 0, o, k).wait_send()
     for block in range(5):
         for o, t in tiles(block):
-            for copy in near(0, o, t) + [near(1, o, t)[1]]:
+            near(1, o, t)[1].wait_send()
+            for copy in near(0, o, t) if block < 2 else [swap(block, o, t)[2]]:
+                copy.wait_send()
+    for e in range(2):
+        for o in range(3):
+            for copy in early(o, e):
                 copy.wait_send()
 
 
@@ -501,7 +555,7 @@
         v((4, 1024, 512)), v((1024, 512)), v((2, 1024, 128), F32), v((64, 32, 128)),
         v((2, 2, 64, 16, 128)), v((2, 2, 1024, 128), F32), v((2, 8, 128), F32),
         v((8, 128, 128), F32), v((2, 128, 128), F32), v((256, 1024)), v((256, 1024)),
-        v((1024, 256)), v((1024, 256)), v((4, 256, 512)), v((4, 256, 512), F32),
+        v((4, 4, 4, 16, 256)), v((4, 4, 4, 16, 256)), v((4, 256, 512)), v((4, 256, 512), F32),
         v((8, 128, 128)), v((8, 128, 128), F32), v((256, 512), F32), v((256, 512), F32),
         v((2, 256, 128), F32), v((256, 512)), v((256, 512)), v((4, 256, 512)),
     ]
@@ -515,11 +569,13 @@
     scratch += [v((3, n, 16, 128)) for n in COUNT]
     scratch += [
         v((20, 16, 128), F32), v((20, 8, 128), F32), v((2, 2, 2, 64, 1024), F32),
-        v((2, 2, 64, 1024), F32), v((64, 32, 128)),
+        v((2, 2, 64, 1024), F32), v((64, 32, 128)), v((3, 2, 2, 4, 4, 16, 256)),
+        v((20, 256, 128)),
     ]
     scratch += [dma((6,)), dma((5,)), dma((8,)), dma((8,)), dma((8,)), dma((8,))]
     scratch += [dma, dma, dma, dma, dma((60,)), dma((60,)), dma((45,)), dma((45,))]
     scratch += [dma((9,)), dma((9,)), dma, dma, dma((2,)), dma((2,)), dma((4,)), dma((4,))]
+    scratch += [dma((12,)), dma((12,))]
     results = pl.pallas_call(
             kernel,
             out_shape=(

time: 65.5 us -> 64.1 us (0.979)
  Pallas kernels: 63.4 us -> 62 us
    pallas_call x1, Pallas kernels: 61.5 us -> 60.1 us  [body(): pl.pallas_call(kernel, out_shape=(jax.ShapeDtypeStruct((128, 1024), BF16)...]
where the time goes in v4:
time: 64.1 us; the launch traced here: 63.9 us
  Pallas kernels  62 us (97%)
  between operations  1.93 us (3%)
    pallas_call x1, Pallas kernels, body(): pl.pallas_call(kernel, out_shape=(jax.ShapeDtypeStruct((128, 1024), BF16)...  60.1 us
    pallas_call x1, Pallas kernels, body(): pl.pallas_call(hand_over, out_shape=tuple((jax.ShapeDtypeStruct(r.shape,...  1.92 us

profile of v4, /device:TPU:1, one launch (start us, length us, event | category | flops | bytes accessed | tf_op | source)
XLA Modules:
  0.0 63.9 jit_solution(17088821727226486990)
XLA Ops:
  1.9 60.1 %shard_map.129 = (bf16[128,1024]{1,0:T(8,128)(2,1)}, bf16[128,1024]{1,0:T(8,128)(2,1)}, f32[8,4096]{1,0:T(8,128)}, f32[8,1024]{1,0:T(8,128)}) custom-call(bf16[128,1024]{1,0:T(8,128)(2,1)} %tok_in.1, bf16[128,1024]{1,0:T(8,128)(2,1)} %gout_in.1, bf16[1024,4096]{1,0:T(8,128)(2,1)} %w_in.1, bf16[1024,1024]{1,0:T(8,128)(2,1)} %w_out.1, f32[8,16]{1,0:T(8,128)} %relb_in.1, ...), custom_call_target="tpu_custom_call" | custom-call | tf_op jit(solution)/shard_map/pallas_call | solution.py:579
  62.0 1.9 %shard_map.130 = (bf16[128,1024]{1,0:T(8,128)(2,1)}, bf16[128,1024]{1,0:T(8,128)(2,1)}, f32[8,4096]{1,0:T(8,128)}, f32[8,1024]{1,0:T(8,128)}) custom-call(bf16[128,1024]{1,0:T(8,128)(2,1)} %get-tuple-element.8.refs_0_, bf16[128,1024]{1,0:T(8,128)(2,1)} %get-tuple-element.9.refs_1_, f32[8,4096]{1,0:T(8,128)} %get-tuple-element.10.refs_2_, ...), custom_call_target="tpu_custom_call" | custom-call | tf_op jit(solution)/shard_map/pallas_call | solution.py:597

commit v5 on v4

--- a/solution.py
+++ b/solution.py
@@ -12,6 +12,7 @@
 MESH = pl.DeviceIdType.MESH
 ORDERS = ((0, 0, 1, 2), (0, 1, 1, 2), (0, 1, 2, 2), (0, 0, 1, 2), (0, 1, 1, 2))
 COUNT = tuple(sum(row.count(o) for row in ORDERS) for o in range(3))
+PAIRS = tuple((n + 1) // 2 for n in COUNT)
 
 
 def slots(block, order):
@@ -28,13 +29,13 @@
     out, gx, gw1, gw2,
     tok, gout, relb, srow, rplace, stamps, wi, wo, sf, sa, rg, rf, meta, bias, mask, xv, gv, xt, gt, act, slp, pw, ps, mix, gg,
     stat, ga, gm, gp, b0, b1, b2, r10, r11, r12, h0, h1, h2, n0, n1, n2, s10, s11, s12, r20, r21, r22, s20, s21, s22,
-    r30, r31, r32, fin, rfin, part, rpart, rz, xn, yn,
+    r30, r31, r32, k20, k21, k22, part, rpart, rz, xn, yn,
     in_sem, wsem, a_s, a_r, c_s, c_r, m_s, m_r, t_s, t_r, p1_s, p1_r, p2_s, p2_r, p3_s, p3_r,
-    f_s, f_r, q_s, q_r, z_s, z_r, e_s, e_r,
+    q_s, q_r, z_s, z_r, e_s, e_r,
 ):
     bs, r1, s1, r2 = (b0, b1, b2), (r10, r11, r12), (s10, s11, s12), (r20, r21, r22)
     halves, nears = (h0, h1, h2), (n0, n1, n2)
-    s2, r3 = (s20, s21, s22), (r30, r31, r32)
+    s2, r3, k2 = (s20, s21, s22), (r30, r31, r32), (k20, k21, k22)
     me = lax.axis_index("seq")
     c = lax.rem(me, 2)
     y = lax.rem(me // 2, 4)
@@ -66,6 +67,11 @@
     barrier = pltpu.get_barrier_semaphore()
 
     pl.semaphore_signal(barrier, inc=1, device_id=(mate,), device_id_type=MESH)
+    for axis in range(3):
+        for k in range(1, 4):
+            pl.semaphore_signal(
+                barrier, inc=1, device_id=(along(axis, k)[1] + mate - me,), device_id_type=MESH
+            )
 
     @pl.loop(1, 64)
     def _(k):
@@ -114,7 +120,7 @@
     picked = dot(pick, tok[...])
     fold(lambda at, cols: picked[at, cols], 0)
 
-    pl.semaphore_wait(barrier, 64)
+    pl.semaphore_wait(barrier, 73)
 
     def peer(i, j):
         there = lax.rem(x + i, 4) * 16 + lax.rem(z * 4 + y + j, 16)
@@ -329,16 +335,20 @@
             ]
         return two, rcopy(halves[o].at[t], nears[o].at[t], *sems[2], dev2)
 
+    def column(block, o, t):
+        return [j for j in range(4) if ORDERS[block][j] == o][t - slots(block, o)[0]]
+
     def swap(block, o, t):
-        j = [j for j in range(4) if ORDERS[block][j] == o][t - slots(block, o)[0]]
         i = sum(COUNT[:o]) + t
-        mine, theirs = gp.at[block - 1, :, pl.ds(128 * j, 128)], yn.at[i]
+        mine = gp.at[block - 1, :, pl.ds(128 * column(block, o, t), 128)]
+        theirs = yn.at[i]
         return mine, theirs, rcopy(mine, theirs, p1_s.at[3 * i], p1_r.at[3 * i], pair(o, t % 2)[4])
 
-    def near_send(block):
+    def near_send(block, columns=(0, 1, 2, 3)):
         for o, t in tiles(block):
-            for copy in near(0, o, t) if block < 2 else [swap(block, o, t)[2]]:
-                copy.start()
+            if column(block, o, t) in columns:
+                for copy in near(0, o, t) if block < 2 else [swap(block, o, t)[2]]:
+                    copy.start()
 
     came = set()
 
@@ -380,32 +390,50 @@
                 value = value + r1[o][t, 0].astype(F32)
             s1[o][t] = value.astype(BF16)
 
-    def hop(stage, block, o, k):
-        there, dev = along((o + stage) % 3, k)
-        if stage == 1:
-            start, count = slots(block, o)
-            at = pl.ds(start, count)
-            i = (block * 3 + o) * 3 + k - 1
-            return rcopy(s1[o].at[at, there], r2[o].at[k - 1, at], p2_s.at[i], p2_r.at[i], dev)
-        i = o * 3 + k - 1
-        return rcopy(s2[o].at[:, there], r3[o].at[k - 1], p3_s.at[i], p3_r.at[i], dev)
+    def hop(block, o, k):
+        there, dev = along((o + 1) % 3, k)
+        start, count = slots(block, o)
+        at = pl.ds(start, count)
+        i = (block * 3 + o) * 3 + k - 1
+        return rcopy(s1[o].at[at, there], r2[o].at[k - 1, at], p2_s.at[i], p2_r.at[i], dev)
+
+    def pack():
+        for o in range(3):
+            for core in range(2):
+                for n in range(PAIRS[o]):
+                    rows8 = [
+                        s2[o][min(i, COUNT[o] - 1), :, 8 * core : 8 * core + 8]
+                        for i in (2 * n, 2 * n + 1)
+                    ]
+                    k2[o][:, core, n] = jnp.concatenate(rows8, axis=1).astype(BF16)
+
+    def last(o, k, rel, sending=True):
+        there, dev = along((o + 2) % 3, k)
+        i = (o * 4 + k) * 2 + rel
+        mine, far = (c, 1 - c) if rel else (c, c)
+        dst = r3[o].at[mine if sending else far, k]
+        return rcopy(
+            k2[o].at[there, far], dst, p3_s.at[i], p3_r.at[i], dev + mate - me if rel else dev
+        )
+
+    lasts = [(o, k, rel) for k in (2, 1, 3, 0) for o in range(3) for rel in range(2) if k or rel]
 
     def far_send(block):
         near_add(block)
         for k in (2, 1, 3):
             for o in range(3):
-                hop(1, block, o, k).start()
+                hop(block, o, k).start()
 
     def far_add(block):
         for o in range(3):
             for k in range(1, 4):
-                hop(1, block, o, k).wait_recv()
+                hop(block, o, k).wait_recv()
             start, count = slots(block, o)
             at = slice(start, start + count)
             value = s1[o][at, coords[(o + 1) % 3]].astype(F32)
             for k in range(3):
                 value = value + r2[o][k, at].astype(F32)
-            s2[o][at] = value.astype(BF16)
+            s2[o][at] = value
 
     product(0, gt, ga[...])
     near_send(0)
@@ -429,7 +457,7 @@
 
     across(0).start()
 
-    for o, h in heads:
+    for h, o in [(h, o) for h in range(4) for o in range(2)]:
         here = (slice(128 * o, 128 * o + 128), slice(128 * h, 128 * h + 128))
         v, q, k = (act[(f,) + here] for f in (1, 2, 3))
         gmh, w = gm[here], pw[4 * o + h]
@@ -443,9 +471,9 @@
             gp[(f,) + here] = (
                 grads[f - 1].astype(BF16).astype(F32) * slp[(f,) + here]
             ).astype(BF16)
-
-    for block in range(2, 5):
-        near_send(block)
+        if o == 1 and h % 2 == 1:
+            for block in range(2, 5):
+                near_send(block, (h - 1, h))
     near_pass(0)
     near_pass(1)
     back = dot(gp[0], wi[0], ((1,), (1,)))
@@ -466,23 +494,9 @@
     rz[chip] = sa[chip]
     for block in range(5):
         far_add(block)
-    for k in (2, 1, 3):
-        for o in range(3):
-            hop(2, 0, o, k).start()
-    for o in range(3):
-        for k in range(1, 4):
-            hop(2, 0, o, k).wait_recv()
-        value = s2[o][:, coords[(o + 2) % 3]].astype(F32)
-        for k in range(3):
-            value = value + r3[o][k].astype(F32)
-        for block in range(5):
-            start, _ = slots(block, o)
-            mine = [j for j in range(4) if ORDERS[block][j] == o]
-            for n, j in enumerate(mine):
-                fin[4 * block + j] = value[start + n]
-    away, home = pl.multiple_of(8 * (1 - c), 8), pl.multiple_of(8 * c, 8)
-    last = rcopy(fin.at[:, pl.ds(away, 8)], rfin, f_s, f_r, mate)
-    last.start()
+    pack()
+    for step in lasts:
+        last(*step).start()
     unpick = jnp.where(to_row(wanted) == rows.astype(F32), 1.0, 0.0).astype(BF16)
 
     for i in range(4):
@@ -497,17 +511,24 @@
     out[...] = (tok[...].astype(F32) + returned(0)).astype(BF16)
     gx[...] = returned(1).astype(BF16)
 
+    for o, k, rel in lasts:
+        last(o, k, rel, False).wait_recv()
     other = pl.multiple_of(512 - half, 512)
-    mine = fin[:, pl.ds(home, 8)]
-    for j in range(4):
-        gw2[:, pl.ds(half + 128 * j, 128)] = mine[j]
-        for f in range(4):
-            gw1[:, pl.ds(f * 1024 + half + 128 * j, 128)] = mine[4 + 4 * f + j]
-    last.wait_recv()
-    for j in range(4):
-        gw2[:, pl.ds(other + 128 * j, 128)] = rfin[j]
-        for f in range(4):
-            gw1[:, pl.ds(f * 1024 + other + 128 * j, 128)] = rfin[4 + 4 * f + j]
+    for o in range(3):
+        here = coords[(o + 2) % 3]
+        for side, base in ((c, half), (1 - c, other)):
+            first_term = k2[o][here, c] if base is half else r3[o][side, 0]
+            value = first_term.astype(F32)
+            for k in range(1, 4):
+                value = value + r3[o][side, k].astype(F32)
+            for block in range(5):
+                for t in range(slots(block, o)[0], sum(slots(block, o))):
+                    tile = value[t // 2, 8 * (t % 2) : 8 * (t % 2) + 8]
+                    at = 128 * column(block, o, t)
+                    if block == 0:
+                        gw2[:, pl.ds(base + at, 128)] = tile
+                    else:
+                        gw1[:, pl.ds((block - 1) * 1024 + base + at, 128)] = tile
 
     for i in range(4):
         scattered(rz, z_s, z_r, i).wait_send()
@@ -517,12 +538,12 @@
         across(kind).wait_send()
     meta_copy.wait_send()
     stat_copy.wait_send()
-    last.wait_send()
+    for step in lasts:
+        last(*step).wait_send()
     for k in range(1, 4):
         for o in range(3):
             for block in range(5):
-                hop(1, block, o, k).wait_send()
-            hop(2, 0, o, k).wait_send()
+                hop(block, o, k).wait_send()
     for block in range(5):
         for o, t in tiles(block):
             near(1, o, t)[1].wait_send()
@@ -565,16 +586,17 @@
     scratch += [v((n, 4, 4, 16, 128)) for n in COUNT]
     scratch += [v((n, 4, 4, 16, 128)) for n in COUNT]
     scratch += [v((3, n, 4, 16, 128)) for n in COUNT]
-    scratch += [v((n, 4, 16, 128)) for n in COUNT]
-    scratch += [v((3, n, 16, 128)) for n in COUNT]
+    scratch += [v((n, 4, 16, 128), F32) for n in COUNT]
+    scratch += [v((2, 4, n, 16, 128)) for n in PAIRS]
+    scratch += [v((4, 2, n, 16, 128)) for n in PAIRS]
     scratch += [
-        v((20, 16, 128), F32), v((20, 8, 128), F32), v((2, 2, 2, 64, 1024), F32),
+        v((2, 2, 2, 64, 1024), F32),
         v((2, 2, 64, 1024), F32), v((64, 32, 128)), v((3, 2, 2, 4, 4, 16, 256)),
         v((20, 256, 128)),
     ]
     scratch += [dma((6,)), dma((5,)), dma((8,)), dma((8,)), dma((8,)), dma((8,))]
     scratch += [dma, dma, dma, dma, dma((60,)), dma((60,)), dma((45,)), dma((45,))]
-    scratch += [dma((9,)), dma((9,)), dma, dma, dma((2,)), dma((2,)), dma((4,)), dma((4,))]
+    scratch += [dma((24,)), dma((24,)), dma((2,)), dma((2,)), dma((4,)), dma((4,))]
     scratch += [dma((12,)), dma((12,))]
     results = pl.pallas_call(
             kernel,

time: 64.1 us -> 62.8 us (0.980)
  Pallas kernels: 62 us -> 60.7 us
    pallas_call x1, Pallas kernels: 60.1 us -> 58.8 us  [body(): pl.pallas_call(kernel, out_shape=(jax.ShapeDtypeStruct((128, 1024), BF16)...]
where the time goes in v5:
time: 62.8 us; the launch traced here: 62.6 us
  Pallas kernels  60.7 us (97%)
  between operations  1.93 us (3%)
    pallas_call x1, Pallas kernels, body(): pl.pallas_call(kernel, out_shape=(jax.ShapeDtypeStruct((128, 1024), BF16)...  58.8 us
    pallas_call x1, Pallas kernels, body(): pl.pallas_call(hand_over, out_shape=tuple((jax.ShapeDtypeStruct(r.shape,...  1.92 us

profile of v5, /device:TPU:1, one launch (start us, length us, event | category | flops | bytes accessed | tf_op | source)
XLA Modules:
  0.0 62.6 jit_solution(13212083845452719806)
XLA Ops:
  1.9 58.8 %shard_map.129 = (bf16[128,1024]{1,0:T(8,128)(2,1)}, bf16[128,1024]{1,0:T(8,128)(2,1)}, f32[8,4096]{1,0:T(8,128)}, f32[8,1024]{1,0:T(8,128)}) custom-call(bf16[128,1024]{1,0:T(8,128)(2,1)} %tok_in.1, bf16[128,1024]{1,0:T(8,128)(2,1)} %gout_in.1, bf16[1024,4096]{1,0:T(8,128)(2,1)} %w_in.1, bf16[1024,1024]{1,0:T(8,128)(2,1)} %w_out.1, f32[8,16]{1,0:T(8,128)} %relb_in.1, ...), custom_call_target="tpu_custom_call" | custom-call | tf_op jit(solution)/shard_map/pallas_call | solution.py:601
  60.7 1.9 %shard_map.130 = (bf16[128,1024]{1,0:T(8,128)(2,1)}, bf16[128,1024]{1,0:T(8,128)(2,1)}, f32[8,4096]{1,0:T(8,128)}, f32[8,1024]{1,0:T(8,128)}) custom-call(bf16[128,1024]{1,0:T(8,128)(2,1)} %get-tuple-element.8.refs_0_, bf16[128,1024]{1,0:T(8,128)(2,1)} %get-tuple-element.9.refs_1_, f32[8,4096]{1,0:T(8,128)} %get-tuple-element.10.refs_2_, ...), custom_call_target="tpu_custom_call" | custom-call | tf_op jit(solution)/shard_map/pallas_call | solution.py:619

commit v6 on v5

--- a/solution.py
+++ b/solution.py
@@ -485,8 +485,8 @@
     near_pass(3)
     near_pass(4)
     far_send(0)
+    home(0)
     far_send(1)
-    home(0)
     home(1)
     for block in range(2, 5):
         far_send(block)
@@ -556,8 +556,16 @@
 
 
 def hand_over(*refs):
-    for i in range(4):
-        refs[4 + i][...] = refs[i][...]
+    ins, outs, held, (in_sem, out_sem) = refs[:4], refs[4:8], refs[8:12], refs[12:]
+    loads = [pltpu.make_async_copy(ins[i], held[i], in_sem.at[i]) for i in range(4)]
+    stores = [pltpu.make_async_copy(held[i], outs[i], out_sem.at[i]) for i in range(4)]
+    for load in loads:
+        load.start()
+    for load, store in zip(loads, stores):
+        load.wait()
+        store.start()
+    for store in stores:
+        store.wait()
 
 
 def body(
@@ -619,8 +627,9 @@
     return pl.pallas_call(
         hand_over,
         out_shape=tuple(jax.ShapeDtypeStruct(r.shape, r.dtype) for r in results),
-        in_specs=[vmem] * 4,
-        out_specs=(vmem,) * 4,
+        in_specs=[hbm] * 4,
+        out_specs=(hbm,) * 4,
+        scratch_shapes=[v(r.shape, r.dtype) for r in results] + [dma((4,)), dma((4,))],
     )(*results)
 
 

time: 62.8 us -> 62.6 us (level)
  no operation moved by 1% of the time
where the time goes in v6:
time: 62.6 us; the launch traced here: 62.5 us
  Pallas kernels  60.6 us (97%)
  between operations  1.93 us (3%)
    pallas_call x1, Pallas kernels, body(): pl.pallas_call(kernel, out_shape=(jax.ShapeDtypeStruct((128, 1024), BF16)...  58.7 us
    pallas_call x1, Pallas kernels, body(): pl.pallas_call(hand_over, out_shape=tuple((jax.ShapeDtypeStruct(r.shape,...  1.85 us

profile of v6, /device:TPU:1, one launch (start us, length us, event | category | flops | bytes accessed | tf_op | source)
XLA Modules:
  0.0 62.5 jit_solution(9730289558100708468)
XLA Ops:
  1.9 58.7 %shard_map.129 = (bf16[128,1024]{1,0:T(8,128)(2,1)}, bf16[128,1024]{1,0:T(8,128)(2,1)}, f32[8,4096]{1,0:T(8,128)}, f32[8,1024]{1,0:T(8,128)}) custom-call(bf16[128,1024]{1,0:T(8,128)(2,1)} %tok_in.1, bf16[128,1024]{1,0:T(8,128)(2,1)} %gout_in.1, bf16[1024,4096]{1,0:T(8,128)(2,1)} %w_in.1, bf16[1024,1024]{1,0:T(8,128)(2,1)} %w_out.1, f32[8,16]{1,0:T(8,128)} %relb_in.1, ...), custom_call_target="tpu_custom_call" | custom-call | tf_op jit(solution)/shard_map/pallas_call | solution.py:609
  60.6 1.9 %shard_map.130 = (bf16[128,1024]{1,0:T(8,128)(2,1)}, bf16[128,1024]{1,0:T(8,128)(2,1)}, f32[8,4096]{1,0:T(8,128)}, f32[8,1024]{1,0:T(8,128)}) custom-call(bf16[128,1024]{1,0:T(8,128)(2,1)} %get-tuple-element.8.refs_0_, bf16[128,1024]{1,0:T(8,128)(2,1)} %get-tuple-element.9.refs_1_, f32[8,4096]{1,0:T(8,128)} %get-tuple-element.10.refs_2_, ...), custom_call_target="tpu_custom_call" | custom-call | tf_op jit(solution)/shard_map/pallas_call | solution.py:627
